TPU v7x, 32 devices: a whole 2x2x4 slice. The times are simulated.
32 devices in a mesh: row: 8 (over z, x), period: 4 (over y, core).
Axes of the slice: x: 2, y: 2, z: 4, core: 2. Of those that a mesh axis runs over, the one named last changes fastest.
Arguments:
- codes: int32 [2048, 64], P('row'), may hold values from 0 to 255
- node: int32 [2048], P('row'), may hold values from 0 to 15
- chosen: int32 [16, 32], replicated, may hold values from 0 to 63, all different within a row
- arm: int32 [2048], P('row'), may hold values 0 or 1
- honest: int32 [2048], P('row'), may hold values 0 or 1
- outcome: bfloat16 [2048, 128], P('row', 'period'), may hold values from -8 to 8
Outputs:
- gains: float32 [32, 16, 256], P('row', None, 'period')
- best_gain: float32 [16], replicated
- effect: float32 [16, 128], P(None, 'period')
Inputs may be any that keep to these rules, and one draw needn't show every extreme that they name: Each row of chosen holds 32 different covariate ids.
All inputs are finite; a program needn't handle non-finite values. No bound on the sum of `arm` or of `honest` on one device may be relied on, other than what follows from the above.
Results may differ from a plain program's by a relative error of at most 0.001.
Values may be sent and summed in bfloat16 or wider, within the bound.
No kernel may reach another device: no remote copies, remote signals or barrier semaphores. Data moves between devices by JAX's collectives and lax.ppermute only.
A program may use at most 128 MiB of HBM per device.

v0:
```python
import functools

import jax
import jax.numpy as jnp
from jax import lax
from jax.experimental import pallas as pl
from jax.experimental.pallas import tpu as pltpu
from jax.sharding import PartitionSpec as P

NODES = 16
BINS = 256
LANES = 128
PAIRS = NODES // 2
BF16 = jnp.bfloat16
F32 = jnp.float32
NT = (((1,), (1,)), ((), ()))


def iota(shape, axis):
    return lax.broadcasted_iota(jnp.int32, shape, axis)


def dot(a, b, dims=(((1,), (0,)), ((), ()))):
    return lax.dot_general(a.astype(BF16), b.astype(BF16), dims, preferred_element_type=F32)


def block_rows(weeks, per_owner):
    return -(-(weeks + 8 + per_owner) // 16) * 16


def pack_kernel(owners, codes_ref, node_ref, arm_ref, honest_ref, chosen_ref, outcome_ref, own_ref, away_ref, scratch):
    units, covars = codes_ref.shape
    slots, weeks = chosen_ref.shape[1], outcome_ref.shape[1]
    per_owner = slots // owners
    rows = own_ref.shape[0] - slots // 2
    room = units // PAIRS
    me = lax.axis_index("row")
    node, arm, honest = node_ref[...], arm_ref[...], honest_ref[...]

    before = (iota((units, units), 0) < iota((units, units), 1)).astype(BF16)
    pair = lax.shift_right_logical(node, 1)
    group = iota((PAIRS, units), 0)
    in_pair = ((group == pair) & (honest == 1)).astype(F32)
    held = jnp.minimum(jnp.sum(in_pair, axis=1, keepdims=True), float(room))
    index = jnp.sum(in_pair * dot(in_pair, before), axis=0, keepdims=True)
    placed = (honest == 1) & (index < room)
    filler = jnp.broadcast_to(jnp.where(placed, 0.0, 1.0), (8, units))
    filler_rank = dot(filler, before)[0:1]
    free = jnp.broadcast_to(room - held, (PAIRS, units))
    lower = (iota((PAIRS, PAIRS), 1) < iota((PAIRS, PAIRS), 0)).astype(BF16)
    first = dot(lower, free)
    in_gap = (filler_rank >= first) & (filler_rank < first + free)
    gap_lane = jnp.sum(
        jnp.where(in_gap, group.astype(F32) * room + held - first + filler_rank, 0.0), axis=0, keepdims=True
    )
    lane = jnp.where(placed, pair * room + index.astype(jnp.int32), gap_lane.astype(jnp.int32))
    lane = lane ^ (room * (me & 3))
    place = jnp.where(iota((units, units), 0) == lane, 1.0, 0.0).astype(BF16)

    keys = jnp.concatenate(
        [node.astype(F32), arm.astype(F32), honest.astype(F32), jnp.zeros((5, units), F32)], axis=0
    )
    wide = jnp.concatenate(
        [outcome_ref[...].astype(F32), codes_ref[...].astype(F32), jnp.zeros((units, LANES - weeks - covars), F32)], axis=1
    )
    sorted_wide = dot(jnp.concatenate([wide.T, keys], axis=0), place, NT)
    sorted_keys = sorted_wide[LANES:]

    flat = jnp.concatenate([chosen_ref[n : n + 1, :] for n in range(NODES)], axis=1)
    hot = jnp.where(iota((covars, NODES * slots), 0) == flat, 1.0, 0.0)
    per_node = dot(hot, sorted_wide[weeks : weeks + covars], (((0,), (0,)), ((), ())))
    picked = jnp.zeros((slots, units), F32)
    for n in range(NODES):
        picked = picked + jnp.where(sorted_keys[0:1] == float(n), per_node[n * slots : (n + 1) * slots], 0.0)
    for j in range(owners):
        scratch[j, 0:per_owner] = picked[j * per_owner : (j + 1) * per_owner]

    common = jnp.concatenate(
        [sorted_wide[0:weeks], sorted_keys, jnp.zeros((rows - weeks - 8, units), F32)], axis=0
    ).astype(BF16)
    half = owners // 2
    for start, out in ((0, own_ref), (half, away_ref)):
        mine = jnp.concatenate([scratch[me ^ (start + j)][0:per_owner] for j in range(half)], axis=0)
        out[0:rows] = common
        out[rows:] = mine.astype(BF16)


def gain_kernel(layout, weeks, per_owner, *refs):
    n_in = len(layout)
    blocks = refs[:n_in]
    gain_ref, effect_ref, sums, steps, outs, keys = refs[n_in:]
    depth = outs.shape[2]
    me = lax.axis_index("row")
    where_of = {}
    for ref, (ids, pick_row) in zip(blocks, layout):
        for at, k in enumerate(ids):
            where_of[k] = (ref, at, pick_row)
    n_blocks = len(where_of)
    quarter = lax.shift_right_logical(iota((8, LANES), 1), 5) ^ (me & 3)
    masks = [quarter == t for t in range(4)]
    bins_up = (iota((BINS, depth), 0) + 1).astype(F32).astype(BF16)
    one, zero = jnp.ones((), BF16), jnp.zeros((), BF16)

    def loaded(k, half):
        ref, at, pick_row = where_of[k]
        lanes = slice(half * LANES, (half + 1) * LANES)
        body = ref[at, 0 : weeks + 16, lanes].astype(F32)
        if pick_row == weeks + 8:
            return body
        picks = ref[at, pick_row : pick_row + per_owner, lanes].astype(F32)
        return jnp.concatenate([body[0 : weeks + 8], picks, jnp.zeros((8 - per_owner, LANES), F32)], axis=0)

    def week_rows(g, out, key):
        node, arm, honest = key[0:1], key[1:2], key[2:3]
        rows, counts = [], []
        for m in range(2):
            mine = (node == (2 * g + m).astype(F32)) & (honest == 1.0)
            for a in (1.0, 0.0):
                here = jnp.where(mine & (arm == a), 1.0, 0.0)
                rows.append(out * here)
                counts.append(here)
        counts.append(jnp.zeros((12, out.shape[1]), F32))
        return jnp.concatenate(rows + counts, axis=0).astype(BF16)

    strays = jnp.zeros((1, depth), F32)
    est = jnp.zeros((2 * NODES, weeks), F32)
    est_units = jnp.zeros((2 * NODES, depth), F32)
    for half in range(2):
        held = [loaded(k, half) for k in range(n_blocks)]
        for g in range(half * 4, half * 4 + 4):
            parts = []
            for first in range(0, n_blocks, 4):
                part = held[first]
                for k in range(first + 1, first + 4):
                    mask = jnp.concatenate([masks[(g ^ k) & 3]] * (part.shape[0] // 8), axis=0)
                    part = jnp.where(mask, held[k], part)
                parts.append(part)
            block = jnp.concatenate(parts, axis=1)
            out, key, picks = block[0:weeks], block[weeks : weeks + 8], block[weeks + 8 : weeks + 8 + per_owner]
            outs[g] = out
            keys[g] = key
            node, arm, honest = key[0:1], key[1:2], key[2:3]
            strays = strays + jnp.where((honest == 1.0) & ((node < 2.0 * g) | (node > 2.0 * g + 1.0)), 1.0, 0.0)
            kept = jnp.where(honest == 0.0, node, -1.0)
            kept_hot = kept == iota((NODES, depth), 0).astype(F32)
            hot = jnp.concatenate(
                [jnp.where(kept_hot & (arm == a), 1.0, 0.0) for a in (1.0, 0.0)], axis=0
            )
            est = est + dot(hot, out, NT)
            est_units = est_units + hot
            for s in range(per_owner):
                pick = jnp.broadcast_to(picks[s : s + 1], (16, depth)).astype(BF16)
                pick = jnp.concatenate([pick] * (BINS // 16), axis=0)
                steps[g, s * BINS : (s + 1) * BINS] = jnp.maximum(jnp.minimum(bins_up - pick, one), zero)
            sums[g] = dot(week_rows(jnp.int32(g), out, key), steps[g], NT)

    units = jnp.sum(est_units, axis=1, keepdims=True)
    effect_ref[...] = est[0:NODES] / (units[0:NODES] + 1.0) - est[NODES:] / (units[NODES:] + 1.0)

    @pl.when(jnp.sum(strays) > 0.0)
    def _():
        def over(i, carry):
            g, other = i // PAIRS, i % PAIRS

            @pl.when(g != other)
            def _():
                sums[g] += dot(week_rows(g, outs[other], keys[other]), steps[other], NT)

            return carry

        lax.fori_loop(0, PAIRS * PAIRS, over, 0)

    for g in range(PAIRS):
        for m in range(2):
            base = 2 * m * weeks
            treated, control = sums[g, base : base + weeks], sums[g, base + weeks : base + 2 * weeks]
            counts = sums[g, 4 * weeks + 2 * m : 4 * weeks + 2 * m + 2]
            lt, lc = counts[0:1], counts[1:2]
            last = slice(BINS - 1, BINS)
            rt, rc = lt[:, last] - lt, lc[:, last] - lc
            it, ic = 1.0 / (rt + 1.0), 1.0 / (rc + 1.0)
            gap = (
                treated * (1.0 / (lt + 1.0) + it)
                - control * (1.0 / (lc + 1.0) + ic)
                - (treated[:, last] * it - control[:, last] * ic)
            )
            cl, cr = lt + lc, rt + rc
            balance = cl * cr / ((cl + cr + 1.0) * (cl + cr + 1.0))
            gain_ref[2 * g + m : 2 * g + m + 1] = balance * jnp.sum(gap * gap, axis=0, keepdims=True)


def finish_kernel(a_ref, b_ref, gain_ref, best_ref):
    per_owner, _, share = gain_ref.shape
    at = lax.axis_index("period") * share
    total = a_ref[...] + b_ref[...]
    best = jnp.broadcast_to(jnp.max(total, axis=1, keepdims=True), (NODES, LANES))
    best_ref[...] = best.T[0:1, 0:NODES]
    for s in range(per_owner):
        turned = pltpu.roll(total[:, s * BINS : (s + 1) * BINS], BINS - at, 1)
        gain_ref[s] = turned[:, 0:share]


def shards(codes, node, chosen, arm, honest, outcome):
    units, weeks = outcome.shape
    slots = chosen.shape[1]
    owners, periods = lax.axis_size("row"), lax.axis_size("period")
    per_owner = slots // owners
    rows = block_rows(weeks, per_owner)
    vmem = pl.BlockSpec(memory_space=pltpu.VMEM)

    def swap(x, axis, bit):
        return lax.ppermute(x, axis, [(i, i ^ bit) for i in range(lax.axis_size(axis))])

    packed = jax.ShapeDtypeStruct((rows + slots // 2, units), BF16)
    own, away = pl.pallas_call(
        functools.partial(pack_kernel, owners),
        out_shape=(packed, packed),
        in_specs=[vmem] * 6,
        out_specs=(vmem, vmem),
        scratch_shapes=[pltpu.VMEM((owners, -(-per_owner // 8) * 8, units), F32)],
    )(codes, node.reshape(1, units), arm.reshape(1, units), honest.reshape(1, units), chosen, outcome)

    groups, bit = owners // 2, owners // 2
    held = [(own[None], [0]), (swap(away, "row", bit)[None], [bit])]
    while groups > 4:
        groups, bit = groups // 2, bit // 2
        cut = rows + groups * per_owner
        ids = [k for _, part in held for k in part]
        send = jnp.concatenate([jnp.concatenate([x[:, :rows], x[:, cut:]], axis=1) for x, _ in held], axis=0)
        keep = jnp.concatenate([x[:, :cut] for x, _ in held], axis=0)
        held = [(keep, ids), (swap(send, "row", bit), [k ^ bit for k in ids])]
    ids = [k for _, part in held for k in part]
    layout = [(part, rows) for _, part in held]
    blocks = [x for x, _ in held]
    for k in (3, 2, 1):
        send = jnp.concatenate(
            [
                jnp.concatenate(
                    [
                        x[:, : weeks + 8],
                        x[:, rows + k * per_owner : rows + (k + 1) * per_owner],
                        x[:, weeks + 8 + per_owner : rows],
                    ],
                    axis=1,
                )
                for x, _ in held
            ],
            axis=0,
        )
        blocks.append(swap(send, "row", k))
        layout.append(([i ^ k for i in ids], weeks + 8))

    depth = owners * units // PAIRS
    wide = per_owner * BINS
    gain, effect = pl.pallas_call(
        functools.partial(gain_kernel, layout, weeks, per_owner),
        out_shape=(jax.ShapeDtypeStruct((NODES, wide), F32), jax.ShapeDtypeStruct((NODES, weeks), F32)),
        in_specs=[vmem] * len(blocks),
        out_specs=(vmem, vmem),
        scratch_shapes=[
            pltpu.VMEM((PAIRS, 4 * weeks + 16, wide), F32),
            pltpu.VMEM((PAIRS, wide, depth), BF16),
            pltpu.VMEM((PAIRS, weeks, depth), F32),
            pltpu.VMEM((PAIRS, 8, depth), F32),
        ],
        compiler_params=pltpu.CompilerParams(vmem_limit_bytes=40 * 1024 * 1024),
    )(*blocks)

    bit = 1
    while 2 * bit < periods:
        gain = gain + swap(gain, "period", bit)
        bit *= 2
    gains, best = pl.pallas_call(
        finish_kernel,
        out_shape=(
            jax.ShapeDtypeStruct((per_owner, NODES, BINS // periods), F32),
            jax.ShapeDtypeStruct((1, NODES), F32),
        ),
        in_specs=[vmem, vmem],
        out_specs=(vmem, vmem),
    )(gain, swap(gain, "period", bit))
    bit = 1
    while bit < owners:
        best = jnp.maximum(best, swap(best, "row", bit))
        bit *= 2
    return gains, best.reshape(NODES), effect


def solution(mesh):
    in_specs = (P("row", None), P("row"), P(), P("row"), P("row"), P("row", "period"))
    out_specs = (P("row", None, "period"), P(), P(None, "period"))
    return jax.shard_map(shards, mesh=mesh, in_specs=in_specs, out_specs=out_specs, check_vma=False)
```

profile of v0, /device:TPU:0, one launch (start us, length us, event | category | flops | bytes accessed | tf_op | source)
XLA Modules:
  0.0 43.3 jit_solution(11721270512880239243)
XLA Ops:
  0.6 0.0 copy-start.2
  0.6 1.5 %copy.10.outcome_ref = bf16[256,32]{1,0:T(8,128)(2,1)} copy(bf16[256,32]{0,1:T(8,128)(2,1)} %param.11) | data formatting | bytes 32768 | tf_op args[5]
  2.1 0.0 copy-done.2
  2.1 0.8 %copy.9.codes_ref = s32[256,64]{1,0:T(8,128)} copy(s32[256,64]{0,1:T(8,128)S(1)} %copy-done.2) | data formatting | bytes 131072 | tf_op args[0]
  2.9 2.3 %shard_map.85 = (bf16[64,256]{1,0:T(8,128)(2,1)}, bf16[64,256]{1,0:T(8,128)(2,1)}) custom-call(s32[256,64]{1,0:T(8,128)} %copy.9.codes_ref, s32[1,256]{1,0:T(1,128)} %bitcast.13, s32[1,256]{1,0:T(1,128)} %bitcast.14, s32[1,256]{1,0:T(1,128)} %bitcast.15, s32[16,32]{1,0:T(8,128)} %chosen_ref.1, bf16[256,32]{1,0:T(8,128)(2,1)} %copy.10.outcome_ref), custom_call_target="tpu_custom_call" | custom-call | tf_op jit(solution)/shard_map/pallas_call | solution.py:215
  5.2 4.0 %collective-permute-start = (bf16[64,256]{1,0:T(8,128)(2,1)}, bf16[64,256]{1,0:T(8,128)(2,1)S(1)}, u32[]{:S(2)}, u32[]{:S(2)}) collective-permute-start(bf16[64,256]{1,0:T(8,128)(2,1)} %get-tuple-element.10), channel_id=1, source_target_pairs={{0,16},{4,20},{8,24},{12,28},{16,0},{20,4},{24,8},{28,12},{1,17},{... | collective-permute-start | bytes 98312 | tf_op jit(solution)/shard_map/ppermute | solution.py:212
  9.2 0.8 %fusion.3 = (bf16[1,4,256]{2,1,0:T(4,128)(2,1)S(1)}, bf16[1,4,256]{2,1,0:T(4,128)(2,1)S(1)}, bf16[1,4,256]{2,1,0:T(4,128)(2,1)S(1)}, bf16[1,4,256]{2,1,0:T(4,128)(2,1)S(1)}) fusion(bf16[1,64,256]{2,1,0:T(8,128)(2,1)} %bitcast.7), kind=kLoop, calls=%fused_computation.16 | loop fusion | bytes 16384 | tf_op jit(solution)/shard_map/slice | solution.py:241
  10.0 0.7 %slice.48 = bf16[1,40,256]{2,1,0:T(8,128)(2,1)S(1)} slice(bf16[1,64,256]{2,1,0:T(8,128)(2,1)} %bitcast.8), slice={[0:1], [0:40], [0:256]} | slice | bytes 40960 | tf_op jit(solution)/shard_map/slice | solution.py:240
  10.7 1.0 %collective-permute-done = bf16[64,256]{1,0:T(8,128)(2,1)S(1)} collective-permute-done((bf16[64,256]{1,0:T(8,128)(2,1)}, bf16[64,256]{1,0:T(8,128)(2,1)S(1)}, u32[]{:S(2)}, u32[]{:S(2)}) %collective-permute-start) | collective-permute-done | bytes 32800 | tf_op jit(solution)/shard_map/ppermute | solution.py:212
  11.7 0.0 copy-start
  11.8 1.8 %collective-permute-start.3 = (bf16[2,48,256]{2,1,0:T(8,128)(2,1)S(1)}, bf16[2,48,256]{2,1,0:T(8,128)(2,1)S(1)}, u32[]{:S(2)}, u32[]{:S(2)}) collective-permute-start(bf16[2,48,256]{2,1,0:T(8,128)(2,1)S(1)} %get-tuple-element.15), channel_id=1, source_target_pairs={{0,4},{4,0},{8,12},{12,8},{16,20},{20,16},{24,28},{28,24},{1,5},{5... | collective-permute-start | bytes 147464 | tf_op jit(solution)/shard_map/ppermute | solution.py:212
  13.5 1.3 %collective-permute-start.2 = (bf16[2,48,256]{2,1,0:T(8,128)(2,1)S(1)}, bf16[2,48,256]{2,1,0:T(8,128)(2,1)S(1)}, u32[]{:S(2)}, u32[]{:S(2)}) collective-permute-start(bf16[2,48,256]{2,1,0:T(8,128)(2,1)S(1)} %get-tuple-element.16), channel_id=1, source_target_pairs={{0,8},{4,12},{8,0},{12,4},{16,24},{20,28},{24,16},{28,20},{1,9},{5... | collective-permute-start | bytes 147464 | tf_op jit(solution)/shard_map/ppermute | solution.py:212
  14.9 0.4 %collective-permute-start.1 = (bf16[2,48,256]{2,1,0:T(8,128)(2,1)S(1)}, bf16[2,48,256]{2,1,0:T(8,128)(2,1)S(1)}, u32[]{:S(2)}, u32[]{:S(2)}) collective-permute-start(bf16[2,48,256]{2,1,0:T(8,128)(2,1)S(1)} %get-tuple-element.17), channel_id=1, source_target_pairs={{0,12},{4,8},{8,4},{12,0},{16,28},{20,24},{24,20},{28,16},{1,13},{... | collective-permute-start | bytes 147464 | tf_op jit(solution)/shard_map/ppermute | solution.py:212
  15.3 0.6 %collective-permute-done.3.refs_4_ = bf16[2,48,256]{2,1,0:T(8,128)(2,1)S(1)} collective-permute-done((bf16[2,48,256]{2,1,0:T(8,128)(2,1)S(1)}, bf16[2,48,256]{2,1,0:T(8,128)(2,1)S(1)}, u32[]{:S(2)}, u32[]{:S(2)}) %collective-permute-start.3) | collective-permute-done | bytes 49184 | tf_op jit(solution)/shard_map/ppermute | solution.py:212
  15.9 1.7 %collective-permute-done.2.refs_3_ = bf16[2,48,256]{2,1,0:T(8,128)(2,1)S(1)} collective-permute-done((bf16[2,48,256]{2,1,0:T(8,128)(2,1)S(1)}, bf16[2,48,256]{2,1,0:T(8,128)(2,1)S(1)}, u32[]{:S(2)}, u32[]{:S(2)}) %collective-permute-start.2) | collective-permute-done | bytes 49184 | tf_op jit(solution)/shard_map/ppermute | solution.py:212
  17.6 2.2 %collective-permute-done.1.refs_2_ = bf16[2,48,256]{2,1,0:T(8,128)(2,1)S(1)} collective-permute-done((bf16[2,48,256]{2,1,0:T(8,128)(2,1)S(1)}, bf16[2,48,256]{2,1,0:T(8,128)(2,1)S(1)}, u32[]{:S(2)}, u32[]{:S(2)}) %collective-permute-start.1) | collective-permute-done | bytes 49184 | tf_op jit(solution)/shard_map/ppermute | solution.py:212
  19.9 0.0 copy-done
  19.9 2.7 %shard_map.86 = (f32[16,1024]{1,0:T(8,128)S(1)}, f32[16,32]{1,0:T(8,128)}) custom-call(bf16[1,64,256]{2,1,0:T(8,128)(2,1)S(1)} %bitcast.9, bf16[1,64,256]{2,1,0:T(8,128)(2,1)S(1)} %bitcast.12, bf16[2,48,256]{2,1,0:T(8,128)(2,1)S(1)} %collective-permute-done.1.refs_2_, bf16[2,48,256]{2,1,0:T(8,128)(2,1)S(1)} %collective-permute-done.2.refs_3_, ...), custom_call_target="tpu_custom_call" | custom-call | tf_op jit(solution)/shard_map/pallas_call | solution.py:255
  22.6 0.1 collective-permute-start.4
  22.7 1.2 %collective-permute-done.4 = f32[16,1024]{1,0:T(8,128)S(1)} collective-permute-done((f32[16,1024]{1,0:T(8,128)S(1)}, f32[16,1024]{1,0:T(8,128)S(1)}, u32[]{:S(2)}, u32[]{:S(2)}) %collective-permute-start.4) | collective-permute-done | bytes 65568 | tf_op jit(solution)/shard_map/ppermute | solution.py:212
  23.9 0.0 copy-start.1
  24.0 1.6 %collective-permute-start.5 = (f32[16,1024]{1,0:T(8,128)S(1)}, f32[16,1024]{1,0:T(8,128)S(1)}, u32[]{:S(2)}, u32[]{:S(2)}) collective-permute-start(f32[16,1024]{1,0:T(8,128)S(1)} %add.3.a_ref), channel_id=1, source_target_pairs={{0,2},{1,3},{2,0},{3,1},{4,6},{5,7},{6,4},{7,5},{8,10},{9,11},{10,... | collective-permute-start | bytes 196616 | tf_op jit(solution)/shard_map/ppermute | solution.py:212
  25.5 2.7 %collective-permute-done.5.b_ref = f32[16,1024]{1,0:T(8,128)S(1)} collective-permute-done((f32[16,1024]{1,0:T(8,128)S(1)}, f32[16,1024]{1,0:T(8,128)S(1)}, u32[]{:S(2)}, u32[]{:S(2)}) %collective-permute-start.5) | collective-permute-done | bytes 65568 | tf_op jit(solution)/shard_map/ppermute | solution.py:212
  28.3 0.0 copy-done.1
  28.3 0.0 copy-start.3
  28.3 0.6 %copy-done.3 = f32[16,1024]{1,0:T(8,128)} copy-done((f32[16,1024]{1,0:T(8,128)}, f32[16,1024]{1,0:T(8,128)S(1)}, u32[]{:S(2)}) %copy-start.3) | copy-done | bytes 65560
  28.9 1.7 %shard_map.87 = (f32[4,16,64]{2,1,0:T(8,128)}, f32[1,16]{1,0:T(1,128)}) custom-call(f32[16,1024]{1,0:T(8,128)} %copy-done.1, f32[16,1024]{1,0:T(8,128)} %copy-done.3), custom_call_target="tpu_custom_call" | custom-call | tf_op jit(solution)/shard_map/pallas_call | solution.py:273
  30.6 0.0 copy-start.4
  30.6 0.7 %copy-done.4 = f32[1,16]{1,0:T(1,128)S(1)} copy-done((f32[1,16]{1,0:T(1,128)S(1)}, f32[1,16]{1,0:T(1,128)}, u32[]{:S(2)}) %copy-start.4) | copy-done | bytes 88
  31.2 0.5 %collective-permute-start.6 = (f32[1,16]{1,0:T(1,128)S(1)}, f32[1,16]{1,0:T(1,128)S(1)}, u32[]{:S(2)}, u32[]{:S(2)}) collective-permute-start(f32[1,16]{1,0:T(1,128)S(1)} %copy-done.4), channel_id=1, source_target_pairs={{0,4},{4,0},{8,12},{12,8},{16,20},{20,16},{24,28},{28,24},{1,5},{5... | collective-permute-start | bytes 200 | tf_op jit(solution)/shard_map/ppermute | solution.py:212
  31.8 3.0 %collective-permute-done.6 = f32[1,16]{1,0:T(1,128)S(1)} collective-permute-done((f32[1,16]{1,0:T(1,128)S(1)}, f32[1,16]{1,0:T(1,128)S(1)}, u32[]{:S(2)}, u32[]{:S(2)}) %collective-permute-start.6) | collective-permute-done | bytes 96 | tf_op jit(solution)/shard_map/ppermute | solution.py:212
  34.8 0.7 %collective-permute-start.7 = (f32[1,16]{1,0:T(1,128)S(1)}, f32[1,16]{1,0:T(1,128)S(1)}, u32[]{:S(2)}, u32[]{:S(2)}) collective-permute-start(f32[1,16]{1,0:T(1,128)S(1)} %max.9), channel_id=1, source_target_pairs={{0,8},{4,12},{8,0},{12,4},{16,24},{20,28},{24,16},{28,20},{1,9},{5... | collective-permute-start | bytes 200 | tf_op jit(solution)/shard_map/ppermute | solution.py:212
  35.4 2.9 %collective-permute-done.7 = f32[1,16]{1,0:T(1,128)S(1)} collective-permute-done((f32[1,16]{1,0:T(1,128)S(1)}, f32[1,16]{1,0:T(1,128)S(1)}, u32[]{:S(2)}, u32[]{:S(2)}) %collective-permute-start.7) | collective-permute-done | bytes 96 | tf_op jit(solution)/shard_map/ppermute | solution.py:212
  38.3 2.8 %collective-permute-start.8 = (f32[1,16]{1,0:T(1,128)S(1)}, f32[1,16]{1,0:T(1,128)S(1)}, u32[]{:S(2)}, u32[]{:S(2)}) collective-permute-start(f32[1,16]{1,0:T(1,128)S(1)} %max.10), channel_id=1, source_target_pairs={{0,16},{4,20},{8,24},{12,28},{16,0},{20,4},{24,8},{28,12},{1,17},{... | collective-permute-start | bytes 200 | tf_op jit(solution)/shard_map/ppermute | solution.py:212
  41.1 1.6 %collective-permute-done.8 = f32[1,16]{1,0:T(1,128)S(1)} collective-permute-done((f32[1,16]{1,0:T(1,128)S(1)}, f32[1,16]{1,0:T(1,128)S(1)}, u32[]{:S(2)}, u32[]{:S(2)}) %collective-permute-start.8) | collective-permute-done | bytes 96 | tf_op jit(solution)/shard_map/ppermute | solution.py:212
  42.8 0.5 %maximum_bitcast_fusion = f32[16]{0:T(128)} fusion(f32[1,16]{1,0:T(1,128)S(1)} %max.10, f32[1,16]{1,0:T(1,128)S(1)} %collective-permute-done.8), kind=kLoop, calls=%fused_computation.15 | loop fusion | flops 16 | bytes 192 | tf_op jit(solution)/shard_map/reshape | solution.py:286
  (6 shorter events, 0.0 us)
Async XLA Ops:
  0.6 1.5 %copy-start.2 = (s32[256,64]{0,1:T(8,128)S(1)}, s32[256,64]{0,1:T(8,128)}, u32[]{:S(2)}) copy-start(s32[256,64]{0,1:T(8,128)} %param.6) | copy-start | bytes 196612
  5.2 6.5 %collective-permute-start = (bf16[64,256]{1,0:T(8,128)(2,1)}, bf16[64,256]{1,0:T(8,128)(2,1)S(1)}, u32[]{:S(2)}, u32[]{:S(2)}) collective-permute-start(bf16[64,256]{1,0:T(8,128)(2,1)} %get-tuple-element.10), channel_id=1, source_target_pairs={{0,16},{4,20},{8,24},{12,28},{16,0},{20,4},{24,8},{28,12},{1,17},{... | collective-permute-start | bytes 98312 | tf_op jit(solution)/shard_map/ppermute | solution.py:212
  11.7 8.1 %copy-start = (bf16[64,256]{1,0:T(8,128)(2,1)S(1)}, bf16[64,256]{1,0:T(8,128)(2,1)}, u32[]{:S(2)}) copy-start(bf16[64,256]{1,0:T(8,128)(2,1)} %get-tuple-element.9) | copy-start | bytes 98308
  11.8 4.2 %collective-permute-start.3 = (bf16[2,48,256]{2,1,0:T(8,128)(2,1)S(1)}, bf16[2,48,256]{2,1,0:T(8,128)(2,1)S(1)}, u32[]{:S(2)}, u32[]{:S(2)}) collective-permute-start(bf16[2,48,256]{2,1,0:T(8,128)(2,1)S(1)} %get-tuple-element.15), channel_id=1, source_target_pairs={{0,4},{4,0},{8,12},{12,8},{16,20},{20,16},{24,28},{28,24},{1,5},{5... | collective-permute-start | bytes 147464 | tf_op jit(solution)/shard_map/ppermute | solution.py:212
  13.5 4.1 %collective-permute-start.2 = (bf16[2,48,256]{2,1,0:T(8,128)(2,1)S(1)}, bf16[2,48,256]{2,1,0:T(8,128)(2,1)S(1)}, u32[]{:S(2)}, u32[]{:S(2)}) collective-permute-start(bf16[2,48,256]{2,1,0:T(8,128)(2,1)S(1)} %get-tuple-element.16), channel_id=1, source_target_pairs={{0,8},{4,12},{8,0},{12,4},{16,24},{20,28},{24,16},{28,20},{1,9},{5... | collective-permute-start | bytes 147464 | tf_op jit(solution)/shard_map/ppermute | solution.py:212
  14.9 5.0 %collective-permute-start.1 = (bf16[2,48,256]{2,1,0:T(8,128)(2,1)S(1)}, bf16[2,48,256]{2,1,0:T(8,128)(2,1)S(1)}, u32[]{:S(2)}, u32[]{:S(2)}) collective-permute-start(bf16[2,48,256]{2,1,0:T(8,128)(2,1)S(1)} %get-tuple-element.17), channel_id=1, source_target_pairs={{0,12},{4,8},{8,4},{12,0},{16,28},{20,24},{24,20},{28,16},{1,13},{... | collective-permute-start | bytes 147464 | tf_op jit(solution)/shard_map/ppermute | solution.py:212
  22.6 1.3 %collective-permute-start.4 = (f32[16,1024]{1,0:T(8,128)S(1)}, f32[16,1024]{1,0:T(8,128)S(1)}, u32[]{:S(2)}, u32[]{:S(2)}) collective-permute-start(f32[16,1024]{1,0:T(8,128)S(1)} %get-tuple-element.11), channel_id=1, source_target_pairs={{0,1},{1,0},{2,3},{3,2},{4,5},{5,4},{6,7},{7,6},{8,9},{9,8},{10,11... | collective-permute-start | bytes 196616 | tf_op jit(solution)/shard_map/ppermute | solution.py:212
  23.9 4.3 %copy-start.1 = (f32[16,1024]{1,0:T(8,128)}, f32[16,1024]{1,0:T(8,128)S(1)}, u32[]{:S(2)}) copy-start(f32[16,1024]{1,0:T(8,128)S(1)} %add.3.a_ref) | copy-start | bytes 196612
  24.0 4.3 %collective-permute-start.5 = (f32[16,1024]{1,0:T(8,128)S(1)}, f32[16,1024]{1,0:T(8,128)S(1)}, u32[]{:S(2)}, u32[]{:S(2)}) collective-permute-start(f32[16,1024]{1,0:T(8,128)S(1)} %add.3.a_ref), channel_id=1, source_target_pairs={{0,2},{1,3},{2,0},{3,1},{4,6},{5,7},{6,4},{7,5},{8,10},{9,11},{10,... | collective-permute-start | bytes 196616 | tf_op jit(solution)/shard_map/ppermute | solution.py:212
  28.3 0.6 %copy-start.3 = (f32[16,1024]{1,0:T(8,128)}, f32[16,1024]{1,0:T(8,128)S(1)}, u32[]{:S(2)}) copy-start(f32[16,1024]{1,0:T(8,128)S(1)} %collective-permute-done.5.b_ref) | copy-start | bytes 196612
  30.6 0.7 %copy-start.4 = (f32[1,16]{1,0:T(1,128)S(1)}, f32[1,16]{1,0:T(1,128)}, u32[]{:S(2)}) copy-start(f32[1,16]{1,0:T(1,128)} %get-tuple-element.13) | copy-start | bytes 196
  31.2 3.5 %collective-permute-start.6 = (f32[1,16]{1,0:T(1,128)S(1)}, f32[1,16]{1,0:T(1,128)S(1)}, u32[]{:S(2)}, u32[]{:S(2)}) collective-permute-start(f32[1,16]{1,0:T(1,128)S(1)} %copy-done.4), channel_id=1, source_target_pairs={{0,4},{4,0},{8,12},{12,8},{16,20},{20,16},{24,28},{28,24},{1,5},{5... | collective-permute-start | bytes 200 | tf_op jit(solution)/shard_map/ppermute | solution.py:212
  34.8 3.5 %collective-permute-start.7 = (f32[1,16]{1,0:T(1,128)S(1)}, f32[1,16]{1,0:T(1,128)S(1)}, u32[]{:S(2)}, u32[]{:S(2)}) collective-permute-start(f32[1,16]{1,0:T(1,128)S(1)} %max.9), channel_id=1, source_target_pairs={{0,8},{4,12},{8,0},{12,4},{16,24},{20,28},{24,16},{28,20},{1,9},{5... | collective-permute-start | bytes 200 | tf_op jit(solution)/shard_map/ppermute | solution.py:212
  38.3 4.4 %collective-permute-start.8 = (f32[1,16]{1,0:T(1,128)S(1)}, f32[1,16]{1,0:T(1,128)S(1)}, u32[]{:S(2)}, u32[]{:S(2)}) collective-permute-start(f32[1,16]{1,0:T(1,128)S(1)} %max.10), channel_id=1, source_target_pairs={{0,16},{4,20},{8,24},{12,28},{16,0},{20,4},{24,8},{28,12},{1,17},{... | collective-permute-start | bytes 200 | tf_op jit(solution)/shard_map/ppermute | solution.py:212
where the time goes:
time: 43.6 us; the launch traced here: 43.3 us
  waiting for transfers between devices  17 us (39%)
  starting transfers between devices  13.3 us (31%)
  Pallas kernels  6.74 us (15%)
  local copies, waits for them, and re-layouts  5.02 us (12%)
  between operations  0.71 us (2%)
  other arithmetic  0.55 us (1%)
    ppermute x9, waiting for transfers between devices, swap(): lax.ppermute(x, axis, [(i, i ^ bit) for i in range(lax.axis_size(axis))])  17 us
    ppermute x9, starting transfers between devices, swap(): lax.ppermute(x, axis, [(i, i ^ bit) for i in range(lax.axis_size(axis))])  13.3 us
    unnamed x12, local copies, waits for them, and re-layouts  3.51 us
    pallas_call x1, Pallas kernels, shards(): pl.pallas_call(functools.partial(gain_kernel, layout, weeks, per_owner),...  2.74 us
    pallas_call x1, Pallas kernels, shards(): pl.pallas_call(functools.partial(pack_kernel, owners), out_shape=(packed,...  2.34 us
    pallas_call x1, Pallas kernels, shards(): pl.pallas_call(finish_kernel, out_shape=(jax.ShapeDtypeStruct((per_owner,...  1.66 us
  transfers between devices with their start and end apart: 9, of which 9 were waited for; matrix products, arithmetic and copies ran while one was open for 3% of the time, Pallas kernels for 0%

commit v1 on v0

--- a/solution.py
+++ b/solution.py
@@ -25,12 +25,12 @@
 
 
 def block_rows(weeks, per_owner):
-    return -(-(weeks + 8 + per_owner) // 16) * 16
+    return weeks + -(-(4 + per_owner) // 8) * 8
 
 
 def pack_kernel(owners, codes_ref, node_ref, arm_ref, honest_ref, chosen_ref, outcome_ref, own_ref, away_ref, scratch):
-    units, covars = codes_ref.shape
-    slots, weeks = chosen_ref.shape[1], outcome_ref.shape[1]
+    covars, units = codes_ref.shape
+    slots, weeks = chosen_ref.shape[1], outcome_ref.shape[0]
     per_owner = slots // owners
     rows = own_ref.shape[0] - slots // 2
     room = units // PAIRS
@@ -60,11 +60,9 @@
     keys = jnp.concatenate(
         [node.astype(F32), arm.astype(F32), honest.astype(F32), jnp.zeros((5, units), F32)], axis=0
     )
-    wide = jnp.concatenate(
-        [outcome_ref[...].astype(F32), codes_ref[...].astype(F32), jnp.zeros((units, LANES - weeks - covars), F32)], axis=1
-    )
-    sorted_wide = dot(jnp.concatenate([wide.T, keys], axis=0), place, NT)
-    sorted_keys = sorted_wide[LANES:]
+    wide = jnp.concatenate([outcome_ref[...].astype(F32), codes_ref[...].astype(F32), keys], axis=0)
+    sorted_wide = dot(wide, place, NT)
+    sorted_keys = sorted_wide[weeks + covars :]
 
     flat = jnp.concatenate([chosen_ref[n : n + 1, :] for n in range(NODES)], axis=1)
     hot = jnp.where(iota((covars, NODES * slots), 0) == flat, 1.0, 0.0)
@@ -75,14 +73,14 @@
     for j in range(owners):
         scratch[j, 0:per_owner] = picked[j * per_owner : (j + 1) * per_owner]
 
-    common = jnp.concatenate(
-        [sorted_wide[0:weeks], sorted_keys, jnp.zeros((rows - weeks - 8, units), F32)], axis=0
-    ).astype(BF16)
     half = owners // 2
+    assert rows == weeks + 8
     for start, out in ((0, own_ref), (half, away_ref)):
-        mine = jnp.concatenate([scratch[me ^ (start + j)][0:per_owner] for j in range(half)], axis=0)
-        out[0:rows] = common
-        out[rows:] = mine.astype(BF16)
+        mine = [scratch[me ^ (start + j)][0:per_owner] for j in range(half)]
+        out[0:rows] = jnp.concatenate(
+            [sorted_wide[0:weeks], sorted_keys[0:4], mine[0], sorted_keys[4 + per_owner :]][: 3 + (per_owner < 4)], axis=0
+        ).astype(BF16)
+        out[rows:] = jnp.concatenate(mine, axis=0).astype(BF16)
 
 
 def gain_kernel(layout, weeks, per_owner, *refs):
@@ -91,24 +89,17 @@
     gain_ref, effect_ref, sums, steps, outs, keys = refs[n_in:]
     depth = outs.shape[2]
     me = lax.axis_index("row")
-    where_of = {}
-    for ref, (ids, pick_row) in zip(blocks, layout):
-        for at, k in enumerate(ids):
-            where_of[k] = (ref, at, pick_row)
+    where_of = {k: (ref, at) for ref, ids in zip(blocks, layout) for at, k in enumerate(ids)}
     n_blocks = len(where_of)
+    rows = block_rows(weeks, per_owner)
     quarter = lax.shift_right_logical(iota((8, LANES), 1), 5) ^ (me & 3)
     masks = [quarter == t for t in range(4)]
     bins_up = (iota((BINS, depth), 0) + 1).astype(F32).astype(BF16)
     one, zero = jnp.ones((), BF16), jnp.zeros((), BF16)
 
     def loaded(k, half):
-        ref, at, pick_row = where_of[k]
-        lanes = slice(half * LANES, (half + 1) * LANES)
-        body = ref[at, 0 : weeks + 16, lanes].astype(F32)
-        if pick_row == weeks + 8:
-            return body
-        picks = ref[at, pick_row : pick_row + per_owner, lanes].astype(F32)
-        return jnp.concatenate([body[0 : weeks + 8], picks, jnp.zeros((8 - per_owner, LANES), F32)], axis=0)
+        ref, at = where_of[k]
+        return ref[at, 0:rows, half * LANES : (half + 1) * LANES].astype(F32)
 
     def week_rows(g, out, key):
         node, arm, honest = key[0:1], key[1:2], key[2:3]
@@ -136,7 +127,7 @@
                     part = jnp.where(mask, held[k], part)
                 parts.append(part)
             block = jnp.concatenate(parts, axis=1)
-            out, key, picks = block[0:weeks], block[weeks : weeks + 8], block[weeks + 8 : weeks + 8 + per_owner]
+            out, key, picks = block[0:weeks], block[weeks : weeks + 8], block[weeks + 4 : weeks + 4 + per_owner]
             outs[g] = out
             keys[g] = key
             node, arm, honest = key[0:1], key[1:2], key[2:3]
@@ -186,18 +177,9 @@
             )
             cl, cr = lt + lc, rt + rc
             balance = cl * cr / ((cl + cr + 1.0) * (cl + cr + 1.0))
-            gain_ref[2 * g + m : 2 * g + m + 1] = balance * jnp.sum(gap * gap, axis=0, keepdims=True)
-
-
-def finish_kernel(a_ref, b_ref, gain_ref, best_ref):
-    per_owner, _, share = gain_ref.shape
-    at = lax.axis_index("period") * share
-    total = a_ref[...] + b_ref[...]
-    best = jnp.broadcast_to(jnp.max(total, axis=1, keepdims=True), (NODES, LANES))
-    best_ref[...] = best.T[0:1, 0:NODES]
-    for s in range(per_owner):
-        turned = pltpu.roll(total[:, s * BINS : (s + 1) * BINS], BINS - at, 1)
-        gain_ref[s] = turned[:, 0:share]
+            gain = balance * jnp.sum(gap * gap, axis=0, keepdims=True)
+            for s in range(per_owner):
+                gain_ref[s, 2 * g + m : 2 * g + m + 1] = gain[:, s * BINS : (s + 1) * BINS]
 
 
 def shards(codes, node, chosen, arm, honest, outcome):
@@ -218,43 +200,34 @@
         in_specs=[vmem] * 6,
         out_specs=(vmem, vmem),
         scratch_shapes=[pltpu.VMEM((owners, -(-per_owner // 8) * 8, units), F32)],
-    )(codes, node.reshape(1, units), arm.reshape(1, units), honest.reshape(1, units), chosen, outcome)
+    )(codes.T, node.reshape(1, units), arm.reshape(1, units), honest.reshape(1, units), chosen, outcome.T)
+
+    def part(x, first, last):
+        bins = x[:, rows + first * per_owner : rows + last * per_owner]
+        block = [x[:, : weeks + 4], bins[:, :per_owner], x[:, weeks + 4 + per_owner : rows]]
+        return jnp.concatenate(block + ([bins] if last > first + 1 else []), axis=1)
 
     groups, bit = owners // 2, owners // 2
     held = [(own[None], [0]), (swap(away, "row", bit)[None], [bit])]
     while groups > 4:
         groups, bit = groups // 2, bit // 2
-        cut = rows + groups * per_owner
-        ids = [k for _, part in held for k in part]
-        send = jnp.concatenate([jnp.concatenate([x[:, :rows], x[:, cut:]], axis=1) for x, _ in held], axis=0)
-        keep = jnp.concatenate([x[:, :cut] for x, _ in held], axis=0)
+        ids = [k for _, some in held for k in some]
+        send = jnp.concatenate([part(x, groups, 2 * groups) for x, _ in held], axis=0)
+        keep = jnp.concatenate([x[:, : rows + groups * per_owner] for x, _ in held], axis=0)
         held = [(keep, ids), (swap(send, "row", bit), [k ^ bit for k in ids])]
-    ids = [k for _, part in held for k in part]
-    layout = [(part, rows) for _, part in held]
+    ids = [k for _, some in held for k in some]
+    layout = [some for _, some in held]
     blocks = [x for x, _ in held]
     for k in (3, 2, 1):
-        send = jnp.concatenate(
-            [
-                jnp.concatenate(
-                    [
-                        x[:, : weeks + 8],
-                        x[:, rows + k * per_owner : rows + (k + 1) * per_owner],
-                        x[:, weeks + 8 + per_owner : rows],
-                    ],
-                    axis=1,
-                )
-                for x, _ in held
-            ],
-            axis=0,
-        )
+        send = jnp.concatenate([part(x, k, k + 1) for x, _ in held], axis=0)
         blocks.append(swap(send, "row", k))
-        layout.append(([i ^ k for i in ids], weeks + 8))
+        layout.append([i ^ k for i in ids])
 
     depth = owners * units // PAIRS
     wide = per_owner * BINS
     gain, effect = pl.pallas_call(
         functools.partial(gain_kernel, layout, weeks, per_owner),
-        out_shape=(jax.ShapeDtypeStruct((NODES, wide), F32), jax.ShapeDtypeStruct((NODES, weeks), F32)),
+        out_shape=(jax.ShapeDtypeStruct((per_owner, NODES, BINS), F32), jax.ShapeDtypeStruct((NODES, weeks), F32)),
         in_specs=[vmem] * len(blocks),
         out_specs=(vmem, vmem),
         scratch_shapes=[
@@ -266,24 +239,19 @@
         compiler_params=pltpu.CompilerParams(vmem_limit_bytes=40 * 1024 * 1024),
     )(*blocks)
 
-    bit = 1
-    while 2 * bit < periods:
-        gain = gain + swap(gain, "period", bit)
+    gain = gain + swap(gain, "period", 1)
+    bit = 2
+    while bit < periods:
+        gain = gain + swap(gain, "period", bit | 1)
         bit *= 2
-    gains, best = pl.pallas_call(
-        finish_kernel,
-        out_shape=(
-            jax.ShapeDtypeStruct((per_owner, NODES, BINS // periods), F32),
-            jax.ShapeDtypeStruct((1, NODES), F32),
-        ),
-        in_specs=[vmem, vmem],
-        out_specs=(vmem, vmem),
-    )(gain, swap(gain, "period", bit))
+    share = BINS // periods
+    gains = lax.dynamic_slice_in_dim(gain, lax.axis_index("period") * share, share, 2)
+    best = jnp.max(gain, axis=(0, 2))
     bit = 1
     while bit < owners:
-        best = jnp.maximum(best, swap(best, "row", bit))
+        best = jnp.maximum(best, swap(best, ("row", "period"), bit * periods | 1))
         bit *= 2
-    return gains, best.reshape(NODES), effect
+    return gains, best, effect
 
 
 def solution(mesh):

time: 43.6 us -> 35.5 us (0.81)
  local copies, waits for them, and re-layouts: 5.02 us -> 2.2 us
  waiting for transfers between devices: 17 us -> 14.3 us
  Pallas kernels: 6.74 us -> 5 us
  starting transfers between devices: 13.3 us -> 12.4 us
    unnamed x12 -> x2, local copies, waits for them, and re-layouts: 3.51 us -> 0.01 us
    ppermute x9, waiting for transfers between devices: 17 us -> 14.3 us  [swap(): lax.ppermute(x, axis, [(i, i ^ bit) for i in range(lax.axis_size(axis))])]
    pallas_call x1 -> x0, Pallas kernels: 1.66 us -> none  [shards(): pl.pallas_call(finish_kernel, out_shape=(jax.ShapeDtypeStruct((per_owner,...]
    ppermute x9, starting transfers between devices: 13.3 us -> 12.4 us  [swap(): lax.ppermute(x, axis, [(i, i ^ bit) for i in range(lax.axis_size(axis))])]
    dynamic_slice x0 -> x1, local copies, waits for them, and re-layouts: none -> 0.69 us  [shards(): lax.dynamic_slice_in_dim(gain, lax.axis_index('period') * share, share, 2)]
    max x2 -> x3, other arithmetic: 0.01 us -> 0.52 us  [shards(): best = jnp.maximum(best, swap(best, ('row', 'period'), bit * periods | 1))]
    reshape x1 -> x0, other arithmetic: 0.51 us -> none  [shards(): return (gains, best.reshape(NODES), effect)]
  transfers between devices with their start and end apart: 9 -> 9, of which waited for: 9 -> 9; matrix products, arithmetic and copies ran while one was open for 3% -> 6% of each run, Pallas kernels for 0% -> 0%
where the time goes in v1:
time: 35.5 us; the launch traced here: 35.3 us
  waiting for transfers between devices  14.3 us (40%)
  starting transfers between devices  12.4 us (35%)
  Pallas kernels  5 us (14%)
  local copies, waits for them, and re-layouts  2.2 us (6%)
  between operations  0.69 us (2%)
  other arithmetic  0.67 us (2%)
    ppermute x9, waiting for transfers between devices, swap(): lax.ppermute(x, axis, [(i, i ^ bit) for i in range(lax.axis_size(axis))])  14.3 us
    ppermute x9, starting transfers between devices, swap(): lax.ppermute(x, axis, [(i, i ^ bit) for i in range(lax.axis_size(axis))])  12.4 us
    pallas_call x1, Pallas kernels, shards(): pl.pallas_call(functools.partial(gain_kernel, layout, weeks, per_owner),...  2.75 us
    pallas_call x1, Pallas kernels, shards(): pl.pallas_call(functools.partial(pack_kernel, owners), out_shape=(packed,...  2.25 us
    slice x2, local copies, waits for them, and re-layouts, part(): bins = x[:, rows + first * per_owner:rows + last * per_owner]  0.77 us
    slice x2, local copies, waits for them, and re-layouts, part(): x[:, :weeks + 4]  0.73 us
  transfers between devices with their start and end apart: 9, of which 9 were waited for; matrix products, arithmetic and copies ran while one was open for 6% of the time, Pallas kernels for 0%

profile of v1, /device:TPU:0, one launch (start us, length us, event | category | flops | bytes accessed | tf_op | source)
XLA Modules:
  0.0 35.3 jit_solution(17792301689452406598)
XLA Ops:
  0.6 2.3 %shard_map.85 = (bf16[56,256]{1,0:T(8,128)(2,1)}, bf16[56,256]{1,0:T(8,128)(2,1)}) custom-call(s32[64,256]{1,0:T(8,128)} %bitcast.13, s32[1,256]{1,0:T(1,128)} %bitcast.15, s32[1,256]{1,0:T(1,128)} %bitcast.16, s32[1,256]{1,0:T(1,128)} %bitcast.17, s32[16,32]{1,0:T(8,128)} %chosen_ref.1, bf16[32,256]{1,0:T(8,128)(2,1)} %bitcast.14), custom_call_target="tpu_custom_call" | custom-call | tf_op jit(solution)/shard_map/pallas_call | solution.py:197
  2.9 4.0 %collective-permute-start = (bf16[56,256]{1,0:T(8,128)(2,1)}, bf16[56,256]{1,0:T(8,128)(2,1)S(1)}, u32[]{:S(2)}, u32[]{:S(2)}) collective-permute-start(bf16[56,256]{1,0:T(8,128)(2,1)} %get-tuple-element.8), channel_id=1, source_target_pairs={{0,16},{4,20},{8,24},{12,28},{16,0},{20,4},{24,8},{28,12},{1,17},{... | collective-permute-start | bytes 86024 | tf_op jit(solution)/shard_map/ppermute | solution.py:194
  6.9 0.8 %fusion.4 = (bf16[1,4,256]{2,1,0:T(4,128)(2,1)S(1)}, bf16[1,4,256]{2,1,0:T(4,128)(2,1)S(1)}, bf16[1,4,256]{2,1,0:T(4,128)(2,1)S(1)}) fusion(bf16[1,56,256]{2,1,0:T(8,128)(2,1)} %bitcast.7), kind=kLoop, calls=%fused_computation.11 | loop fusion | bytes 12288 | tf_op jit(solution)/shard_map/slice | solution.py:206
  7.7 0.7 %slice.36 = bf16[1,36,256]{2,1,0:T(8,128)(2,1)S(1)} slice(bf16[1,56,256]{2,1,0:T(8,128)(2,1)} %bitcast.8), slice={[0:1], [0:36], [0:256]} | slice | bytes 36864 | tf_op jit(solution)/shard_map/slice | solution.py:207
  8.4 0.6 %collective-permute-done = bf16[56,256]{1,0:T(8,128)(2,1)S(1)} collective-permute-done((bf16[56,256]{1,0:T(8,128)(2,1)}, bf16[56,256]{1,0:T(8,128)(2,1)S(1)}, u32[]{:S(2)}, u32[]{:S(2)}) %collective-permute-start) | collective-permute-done | bytes 28704 | tf_op jit(solution)/shard_map/ppermute | solution.py:194
  9.0 0.0 copy-start
  9.0 2.9 %collective-permute-start.1 = (bf16[2,40,256]{2,1,0:T(8,128)(2,1)S(1)}, bf16[2,40,256]{2,1,0:T(8,128)(2,1)S(1)}, u32[]{:S(2)}, u32[]{:S(2)}) collective-permute-start(bf16[2,40,256]{2,1,0:T(8,128)(2,1)S(1)} %get-tuple-element.15), channel_id=1, source_target_pairs={{0,12},{4,8},{8,4},{12,0},{16,28},{20,24},{24,20},{28,16},{1,13},{... | collective-permute-start | bytes 122888 | tf_op jit(solution)/shard_map/ppermute | solution.py:194
  11.9 0.6 %collective-permute-start.2 = (bf16[2,40,256]{2,1,0:T(8,128)(2,1)S(1)}, bf16[2,40,256]{2,1,0:T(8,128)(2,1)S(1)}, u32[]{:S(2)}, u32[]{:S(2)}) collective-permute-start(bf16[2,40,256]{2,1,0:T(8,128)(2,1)S(1)} %get-tuple-element.14), channel_id=1, source_target_pairs={{0,8},{4,12},{8,0},{12,4},{16,24},{20,28},{24,16},{28,20},{1,9},{5... | collective-permute-start | bytes 122888 | tf_op jit(solution)/shard_map/ppermute | solution.py:194
  12.6 0.0 collective-permute-start.3
  12.6 1.4 %collective-permute-done.1.refs_2_ = bf16[2,40,256]{2,1,0:T(8,128)(2,1)S(1)} collective-permute-done((bf16[2,40,256]{2,1,0:T(8,128)(2,1)S(1)}, bf16[2,40,256]{2,1,0:T(8,128)(2,1)S(1)}, u32[]{:S(2)}, u32[]{:S(2)}) %collective-permute-start.1) | collective-permute-done | bytes 40992 | tf_op jit(solution)/shard_map/ppermute | solution.py:194
  14.0 1.9 %collective-permute-done.2.refs_3_ = bf16[2,40,256]{2,1,0:T(8,128)(2,1)S(1)} collective-permute-done((bf16[2,40,256]{2,1,0:T(8,128)(2,1)S(1)}, bf16[2,40,256]{2,1,0:T(8,128)(2,1)S(1)}, u32[]{:S(2)}, u32[]{:S(2)}) %collective-permute-start.2) | collective-permute-done | bytes 40992 | tf_op jit(solution)/shard_map/ppermute | solution.py:194
  15.9 0.6 %collective-permute-done.3.refs_4_ = bf16[2,40,256]{2,1,0:T(8,128)(2,1)S(1)} collective-permute-done((bf16[2,40,256]{2,1,0:T(8,128)(2,1)S(1)}, bf16[2,40,256]{2,1,0:T(8,128)(2,1)S(1)}, u32[]{:S(2)}, u32[]{:S(2)}) %collective-permute-start.3) | collective-permute-done | bytes 40992 | tf_op jit(solution)/shard_map/ppermute | solution.py:194
  16.6 0.0 copy-done
  16.6 2.7 %shard_map.86 = (f32[4,16,256]{2,1,0:T(8,128)S(1)}, f32[16,32]{1,0:T(8,128)}) custom-call(bf16[1,56,256]{2,1,0:T(8,128)(2,1)S(1)} %bitcast.9, bf16[1,56,256]{2,1,0:T(8,128)(2,1)S(1)} %bitcast.12, bf16[2,40,256]{2,1,0:T(8,128)(2,1)S(1)} %collective-permute-done.1.refs_2_, bf16[2,40,256]{2,1,0:T(8,128)(2,1)S(1)} %collective-permute-done.2.refs_3_, ...), custom_call_target="tpu_custom_call" | custom-call | tf_op jit(solution)/shard_map/pallas_call | solution.py:228
  19.3 0.1 collective-permute-start.4
  19.4 1.2 %collective-permute-done.4 = f32[4,16,256]{2,1,0:T(8,128)S(1)} collective-permute-done((f32[4,16,256]{2,1,0:T(8,128)S(1)}, f32[4,16,256]{2,1,0:T(8,128)S(1)}, u32[]{:S(2)}, u32[]{:S(2)}) %collective-permute-start.4) | collective-permute-done | bytes 65568 | tf_op jit(solution)/shard_map/ppermute | solution.py:194
  20.7 1.3 %collective-permute-start.5 = (f32[4,16,256]{2,1,0:T(8,128)S(1)}, f32[4,16,256]{2,1,0:T(8,128)S(1)}, u32[]{:S(2)}, u32[]{:S(2)}) collective-permute-start(f32[4,16,256]{2,1,0:T(8,128)S(1)} %add.9), channel_id=1, source_target_pairs={{0,3},{1,2},{2,1},{3,0},{4,7},{5,6},{6,5},{7,4},{8,11},{9,10},{10,... | collective-permute-start | bytes 196616 | tf_op jit(solution)/shard_map/ppermute | solution.py:194
  22.0 2.8 %collective-permute-done.5 = f32[4,16,256]{2,1,0:T(8,128)S(1)} collective-permute-done((f32[4,16,256]{2,1,0:T(8,128)S(1)}, f32[4,16,256]{2,1,0:T(8,128)S(1)}, u32[]{:S(2)}, u32[]{:S(2)}) %collective-permute-start.5) | collective-permute-done | bytes 65568 | tf_op jit(solution)/shard_map/ppermute | solution.py:194
  24.8 0.1 fusion.3
  24.9 0.1 collective-permute-start.6
  25.0 3.0 %collective-permute-done.6 = f32[16]{0:T(128)S(1)} collective-permute-done((f32[16]{0:T(128)S(1)}, f32[16]{0:T(128)S(1)}, u32[]{:S(2)}, u32[]{:S(2)}) %collective-permute-start.6) | collective-permute-done | bytes 96 | tf_op jit(solution)/shard_map/ppermute | solution.py:194
  27.9 1.2 %collective-permute-start.7 = (f32[16]{0:T(128)S(1)}, f32[16]{0:T(128)S(1)}, u32[]{:S(2)}, u32[]{:S(2)}) collective-permute-start(f32[16]{0:T(128)S(1)} %max.9), channel_id=1, source_target_pairs={{0,9},{1,8},{2,11},{3,10},{4,13},{5,12},{6,15},{7,14},{8,1},{9,0},... | collective-permute-start | bytes 200 | tf_op jit(solution)/shard_map/ppermute | solution.py:194
  29.1 1.8 %collective-permute-done.7 = f32[16]{0:T(128)S(1)} collective-permute-done((f32[16]{0:T(128)S(1)}, f32[16]{0:T(128)S(1)}, u32[]{:S(2)}, u32[]{:S(2)}) %collective-permute-start.7) | collective-permute-done | bytes 96 | tf_op jit(solution)/shard_map/ppermute | solution.py:194
  30.9 2.2 %collective-permute-start.8 = (f32[16]{0:T(128)S(1)}, f32[16]{0:T(128)S(1)}, u32[]{:S(2)}, u32[]{:S(2)}) collective-permute-start(f32[16]{0:T(128)S(1)} %max.10), channel_id=1, source_target_pairs={{0,17},{1,16},{2,19},{3,18},{4,21},{5,20},{6,23},{7,22},{8,25},{9,... | collective-permute-start | bytes 200 | tf_op jit(solution)/shard_map/ppermute | solution.py:194
  33.1 0.7 %constant_dynamic-slice_fusion = f32[4,16,64]{2,1,0:T(8,128)} fusion(f32[4,16,256]{2,1,0:T(8,128)S(1)} %get-tuple-element.12, s32[]{:T(128)S(6)} %select_n.3), kind=kLoop, calls=%fused_computation.9 | loop fusion | bytes 32772 | tf_op jit(solution)/shard_map/dynamic_slice | solution.py:248
  33.8 1.0 %collective-permute-done.8 = f32[16]{0:T(128)S(1)} collective-permute-done((f32[16]{0:T(128)S(1)}, f32[16]{0:T(128)S(1)}, u32[]{:S(2)}, u32[]{:S(2)}) %collective-permute-start.8) | collective-permute-done | bytes 96 | tf_op jit(solution)/shard_map/ppermute | solution.py:194
  34.8 0.5 %max.11 = f32[16]{0:T(128)} maximum(f32[16]{0:T(128)S(1)} %max.10, f32[16]{0:T(128)S(1)} %collective-permute-done.8) | non-fusion elementwise | flops 16 | bytes 192 | tf_op jit(solution)/shard_map/max | solution.py:252
  (6 shorter events, 0.0 us)
Async XLA Ops:
  2.9 6.1 %collective-permute-start = (bf16[56,256]{1,0:T(8,128)(2,1)}, bf16[56,256]{1,0:T(8,128)(2,1)S(1)}, u32[]{:S(2)}, u32[]{:S(2)}) collective-permute-start(bf16[56,256]{1,0:T(8,128)(2,1)} %get-tuple-element.8), channel_id=1, source_target_pairs={{0,16},{4,20},{8,24},{12,28},{16,0},{20,4},{24,8},{28,12},{1,17},{... | collective-permute-start | bytes 86024 | tf_op jit(solution)/shard_map/ppermute | solution.py:194
  9.0 7.6 %copy-start = (bf16[56,256]{1,0:T(8,128)(2,1)S(1)}, bf16[56,256]{1,0:T(8,128)(2,1)}, u32[]{:S(2)}) copy-start(bf16[56,256]{1,0:T(8,128)(2,1)} %get-tuple-element.7) | copy-start | bytes 86020
  9.0 5.0 %collective-permute-start.1 = (bf16[2,40,256]{2,1,0:T(8,128)(2,1)S(1)}, bf16[2,40,256]{2,1,0:T(8,128)(2,1)S(1)}, u32[]{:S(2)}, u32[]{:S(2)}) collective-permute-start(bf16[2,40,256]{2,1,0:T(8,128)(2,1)S(1)} %get-tuple-element.15), channel_id=1, source_target_pairs={{0,12},{4,8},{8,4},{12,0},{16,28},{20,24},{24,20},{28,16},{1,13},{... | collective-permute-start | bytes 122888 | tf_op jit(solution)/shard_map/ppermute | solution.py:194
  11.9 4.0 %collective-permute-start.2 = (bf16[2,40,256]{2,1,0:T(8,128)(2,1)S(1)}, bf16[2,40,256]{2,1,0:T(8,128)(2,1)S(1)}, u32[]{:S(2)}, u32[]{:S(2)}) collective-permute-start(bf16[2,40,256]{2,1,0:T(8,128)(2,1)S(1)} %get-tuple-element.14), channel_id=1, source_target_pairs={{0,8},{4,12},{8,0},{12,4},{16,24},{20,28},{24,16},{28,20},{1,9},{5... | collective-permute-start | bytes 122888 | tf_op jit(solution)/shard_map/ppermute | solution.py:194
  12.6 4.0 %collective-permute-start.3 = (bf16[2,40,256]{2,1,0:T(8,128)(2,1)S(1)}, bf16[2,40,256]{2,1,0:T(8,128)(2,1)S(1)}, u32[]{:S(2)}, u32[]{:S(2)}) collective-permute-start(bf16[2,40,256]{2,1,0:T(8,128)(2,1)S(1)} %get-tuple-element.13), channel_id=1, source_target_pairs={{0,4},{4,0},{8,12},{12,8},{16,20},{20,16},{24,28},{28,24},{1,5},{5... | collective-permute-start | bytes 122888 | tf_op jit(solution)/shard_map/ppermute | solution.py:194
  19.3 1.3 %collective-permute-start.4 = (f32[4,16,256]{2,1,0:T(8,128)S(1)}, f32[4,16,256]{2,1,0:T(8,128)S(1)}, u32[]{:S(2)}, u32[]{:S(2)}) collective-permute-start(f32[4,16,256]{2,1,0:T(8,128)S(1)} %get-tuple-element.9), channel_id=1, source_target_pairs={{0,1},{1,0},{2,3},{3,2},{4,5},{5,4},{6,7},{7,6},{8,9},{9,8},{10,11... | collective-permute-start | bytes 196616 | tf_op jit(solution)/shard_map/ppermute | solution.py:194
  20.7 4.1 %collective-permute-start.5 = (f32[4,16,256]{2,1,0:T(8,128)S(1)}, f32[4,16,256]{2,1,0:T(8,128)S(1)}, u32[]{:S(2)}, u32[]{:S(2)}) collective-permute-start(f32[4,16,256]{2,1,0:T(8,128)S(1)} %add.9), channel_id=1, source_target_pairs={{0,3},{1,2},{2,1},{3,0},{4,7},{5,6},{6,5},{7,4},{8,11},{9,10},{10,... | collective-permute-start | bytes 196616 | tf_op jit(solution)/shard_map/ppermute | solution.py:194
  24.9 3.0 %collective-permute-start.6 = (f32[16]{0:T(128)S(1)}, f32[16]{0:T(128)S(1)}, u32[]{:S(2)}, u32[]{:S(2)}) collective-permute-start(f32[16]{0:T(128)S(1)} %get-tuple-element.11), channel_id=1, source_target_pairs={{0,5},{1,4},{2,7},{3,6},{4,1},{5,0},{6,3},{7,2},{8,13},{9,12},{10,... | collective-permute-start | bytes 200 | tf_op jit(solution)/shard_map/ppermute | solution.py:194
  27.9 3.0 %collective-permute-start.7 = (f32[16]{0:T(128)S(1)}, f32[16]{0:T(128)S(1)}, u32[]{:S(2)}, u32[]{:S(2)}) collective-permute-start(f32[16]{0:T(128)S(1)} %max.9), channel_id=1, source_target_pairs={{0,9},{1,8},{2,11},{3,10},{4,13},{5,12},{6,15},{7,14},{8,1},{9,0},... | collective-permute-start | bytes 200 | tf_op jit(solution)/shard_map/ppermute | solution.py:194
  30.9 3.9 %collective-permute-start.8 = (f32[16]{0:T(128)S(1)}, f32[16]{0:T(128)S(1)}, u32[]{:S(2)}, u32[]{:S(2)}) collective-permute-start(f32[16]{0:T(128)S(1)} %max.10), channel_id=1, source_target_pairs={{0,17},{1,16},{2,19},{3,18},{4,21},{5,20},{6,23},{7,22},{8,25},{9,... | collective-permute-start | bytes 200 | tf_op jit(solution)/shard_map/ppermute | solution.py:194

commit v2 on v1

--- a/solution.py
+++ b/solution.py
@@ -86,7 +86,7 @@
 def gain_kernel(layout, weeks, per_owner, *refs):
     n_in = len(layout)
     blocks = refs[:n_in]
-    gain_ref, effect_ref, sums, steps, outs, keys = refs[n_in:]
+    gain_ref, effect_ref, outs, keys, sums = refs[n_in:]
     depth = outs.shape[2]
     me = lax.axis_index("row")
     where_of = {k: (ref, at) for ref, ids in zip(blocks, layout) for at, k in enumerate(ids)}
@@ -103,15 +103,42 @@
 
     def week_rows(g, out, key):
         node, arm, honest = key[0:1], key[1:2], key[2:3]
-        rows, counts = [], []
+        mine, counts = [], []
         for m in range(2):
-            mine = (node == (2 * g + m).astype(F32)) & (honest == 1.0)
+            of_node = (node == (2 * g + m).astype(F32)) & (honest == 1.0)
             for a in (1.0, 0.0):
-                here = jnp.where(mine & (arm == a), 1.0, 0.0)
-                rows.append(out * here)
-                counts.append(here)
-        counts.append(jnp.zeros((12, out.shape[1]), F32))
-        return jnp.concatenate(rows + counts, axis=0).astype(BF16)
+                here = jnp.where(of_node & (arm == a), 1.0, 0.0)
+                mine.append(out * here)
+                counts.append(jnp.broadcast_to(here, (8, here.shape[1])))
+        return jnp.concatenate(mine + counts, axis=0).astype(BF16)
+
+    def step_rows(key, s):
+        pick = jnp.broadcast_to(key[4 + s : 5 + s], (16, key.shape[1])).astype(BF16)
+        pick = jnp.concatenate([pick] * (BINS // 16), axis=0)
+        return jnp.maximum(jnp.minimum(bins_up - pick, one), zero)
+
+    def pair_gains(left, total):
+        gains = []
+        for m in range(2):
+            base, count = 2 * m * weeks, 4 * weeks + 16 * m
+            treated, control = left[base : base + weeks], left[base + weeks : base + 2 * weeks]
+            all_treated, all_control = total[base : base + weeks], total[base + weeks : base + 2 * weeks]
+            lt, lc = left[count : count + 8], left[count + 8 : count + 16]
+            rt, rc = total[count : count + 8] - lt, total[count + 8 : count + 16] - lc
+            it, ic = 1.0 / (rt + 1.0), 1.0 / (rc + 1.0)
+            at, ac = 1.0 / (lt + 1.0) + it, 1.0 / (lc + 1.0) + ic
+            spread = None
+            for w in range(0, weeks, 8):
+                rng = slice(w, w + 8)
+                gap = (treated[rng] * at - all_treated[rng] * it) - (control[rng] * ac - all_control[rng] * ic)
+                spread = gap * gap if spread is None else spread + gap * gap
+            cl, cr = lt + lc, rt + rc
+            balance = cl * cr / ((cl + cr + 1.0) * (cl + cr + 1.0))
+            gains.append(jnp.sum(balance * spread, axis=0, keepdims=True))
+        return gains
+
+    def last_bin(left):
+        return jnp.broadcast_to(left[:, BINS - 1 : BINS], left.shape)
 
     strays = jnp.zeros((1, depth), F32)
     est = jnp.zeros((2 * NODES, weeks), F32)
@@ -127,7 +154,7 @@
                     part = jnp.where(mask, held[k], part)
                 parts.append(part)
             block = jnp.concatenate(parts, axis=1)
-            out, key, picks = block[0:weeks], block[weeks : weeks + 8], block[weeks + 4 : weeks + 4 + per_owner]
+            out, key = block[0:weeks], block[weeks : weeks + 8]
             outs[g] = out
             keys[g] = key
             node, arm, honest = key[0:1], key[1:2], key[2:3]
@@ -139,47 +166,34 @@
             )
             est = est + dot(hot, out, NT)
             est_units = est_units + hot
+            mine = week_rows(jnp.int32(g), out, key)
+            total = None
             for s in range(per_owner):
-                pick = jnp.broadcast_to(picks[s : s + 1], (16, depth)).astype(BF16)
-                pick = jnp.concatenate([pick] * (BINS // 16), axis=0)
-                steps[g, s * BINS : (s + 1) * BINS] = jnp.maximum(jnp.minimum(bins_up - pick, one), zero)
-            sums[g] = dot(week_rows(jnp.int32(g), out, key), steps[g], NT)
+                left = dot(mine, step_rows(key, s), NT)
+                total = last_bin(left) if total is None else total
+                for m, gain in enumerate(pair_gains(left, total)):
+                    gain_ref[s, 2 * g + m : 2 * g + m + 1] = gain
 
     units = jnp.sum(est_units, axis=1, keepdims=True)
-    effect_ref[...] = est[0:NODES] / (units[0:NODES] + 1.0) - est[NODES:] / (units[NODES:] + 1.0)
+    effect_ref[...] = est / (units + 1.0)
 
     @pl.when(jnp.sum(strays) > 0.0)
     def _():
-        def over(i, carry):
-            g, other = i // PAIRS, i % PAIRS
-
-            @pl.when(g != other)
-            def _():
-                sums[g] += dot(week_rows(g, outs[other], keys[other]), steps[other], NT)
-
+        def over_pairs(g, carry):
+            for s in range(per_owner):
+                sums[...] = jnp.zeros_like(sums)
+
+                def over_lanes(other, carry):
+                    sums[...] += dot(week_rows(g, outs[other], keys[other]), step_rows(keys[other], s), NT)
+                    return carry
+
+                lax.fori_loop(0, PAIRS, over_lanes, 0)
+                left = sums[...]
+                for m, gain in enumerate(pair_gains(left, last_bin(left))):
+                    gain_ref[s, pl.ds(2 * g + m, 1)] = gain
             return carry
 
-        lax.fori_loop(0, PAIRS * PAIRS, over, 0)
-
-    for g in range(PAIRS):
-        for m in range(2):
-            base = 2 * m * weeks
-            treated, control = sums[g, base : base + weeks], sums[g, base + weeks : base + 2 * weeks]
-            counts = sums[g, 4 * weeks + 2 * m : 4 * weeks + 2 * m + 2]
-            lt, lc = counts[0:1], counts[1:2]
-            last = slice(BINS - 1, BINS)
-            rt, rc = lt[:, last] - lt, lc[:, last] - lc
-            it, ic = 1.0 / (rt + 1.0), 1.0 / (rc + 1.0)
-            gap = (
-                treated * (1.0 / (lt + 1.0) + it)
-                - control * (1.0 / (lc + 1.0) + ic)
-                - (treated[:, last] * it - control[:, last] * ic)
-            )
-            cl, cr = lt + lc, rt + rc
-            balance = cl * cr / ((cl + cr + 1.0) * (cl + cr + 1.0))
-            gain = balance * jnp.sum(gap * gap, axis=0, keepdims=True)
-            for s in range(per_owner):
-                gain_ref[s, 2 * g + m : 2 * g + m + 1] = gain[:, s * BINS : (s + 1) * BINS]
+        lax.fori_loop(0, PAIRS, over_pairs, 0)
 
 
 def shards(codes, node, chosen, arm, honest, outcome):
@@ -194,13 +208,15 @@
         return lax.ppermute(x, axis, [(i, i ^ bit) for i in range(lax.axis_size(axis))])
 
     packed = jax.ShapeDtypeStruct((rows + slots // 2, units), BF16)
+    inputs = (codes.T, node.reshape(1, units), arm.reshape(1, units), honest.reshape(1, units), chosen, outcome.T)
     own, away = pl.pallas_call(
         functools.partial(pack_kernel, owners),
         out_shape=(packed, packed),
         in_specs=[vmem] * 6,
         out_specs=(vmem, vmem),
+        compiler_params=pltpu.CompilerParams(vmem_limit_bytes=8 * 1024 * 1024),
         scratch_shapes=[pltpu.VMEM((owners, -(-per_owner // 8) * 8, units), F32)],
-    )(codes.T, node.reshape(1, units), arm.reshape(1, units), honest.reshape(1, units), chosen, outcome.T)
+    )(*(pltpu.with_memory_space_constraint(x, pltpu.HBM) for x in inputs))
 
     def part(x, first, last):
         bins = x[:, rows + first * per_owner : rows + last * per_owner]
@@ -224,19 +240,17 @@
         layout.append([i ^ k for i in ids])
 
     depth = owners * units // PAIRS
-    wide = per_owner * BINS
     gain, effect = pl.pallas_call(
         functools.partial(gain_kernel, layout, weeks, per_owner),
-        out_shape=(jax.ShapeDtypeStruct((per_owner, NODES, BINS), F32), jax.ShapeDtypeStruct((NODES, weeks), F32)),
+        out_shape=(jax.ShapeDtypeStruct((per_owner, NODES, BINS), F32), jax.ShapeDtypeStruct((2 * NODES, weeks), F32)),
         in_specs=[vmem] * len(blocks),
         out_specs=(vmem, vmem),
         scratch_shapes=[
-            pltpu.VMEM((PAIRS, 4 * weeks + 16, wide), F32),
-            pltpu.VMEM((PAIRS, wide, depth), BF16),
             pltpu.VMEM((PAIRS, weeks, depth), F32),
             pltpu.VMEM((PAIRS, 8, depth), F32),
+            pltpu.VMEM((4 * weeks + 32, BINS), F32),
         ],
-        compiler_params=pltpu.CompilerParams(vmem_limit_bytes=40 * 1024 * 1024),
+        compiler_params=pltpu.CompilerParams(vmem_limit_bytes=16 * 1024 * 1024),
     )(*blocks)
 
     gain = gain + swap(gain, "period", 1)
@@ -251,7 +265,7 @@
     while bit < owners:
         best = jnp.maximum(best, swap(best, ("row", "period"), bit * periods | 1))
         bit *= 2
-    return gains, best, effect
+    return gains, best, effect[:NODES] - effect[NODES:]
 
 
 def solution(mesh):

time: 35.5 us -> 34 us (0.958)
  local copies, waits for them, and re-layouts: 2.2 us -> 0.71 us
  Pallas kernels: 5 us -> 3.73 us
  waiting for transfers between devices: 14.3 us -> 15 us
  other arithmetic: 0.67 us -> 1.27 us
    slice x2, local copies, waits for them, and re-layouts: 0.77 us -> 0.01 us  [part(): bins = x[:, rows + first * per_owner:rows + last * per_owner]]
    slice x2, local copies, waits for them, and re-layouts: 0.73 us -> 0.01 us  [part(): x[:, :weeks + 4]]
    ppermute x9, waiting for transfers between devices: 14.3 us -> 15 us  [swap(): lax.ppermute(x, axis, [(i, i ^ bit) for i in range(lax.axis_size(axis))])]
    pallas_call x1, Pallas kernels: 2.75 us -> 2.09 us  [shards(): pl.pallas_call(functools.partial(gain_kernel, layout, weeks, per_owner),...]
    pallas_call x1, Pallas kernels: 2.25 us -> 1.63 us  [shards(): pl.pallas_call(functools.partial(pack_kernel, owners), out_shape=(packed,...]
    sub x0 -> x1, other arithmetic: none -> 0.6 us  [shards(): return (gains, best, effect[:NODES] - effect[NODES:])]
  transfers between devices with their start and end apart: 9 -> 9, of which waited for: 9 -> 9; matrix products, arithmetic and copies ran while one was open for 6% -> 4% of each run, Pallas kernels for 0% -> 0%
where the time goes in v2:
time: 34 us; the launch traced here: 33.8 us
  waiting for transfers between devices  15 us (44%)
  starting transfers between devices  12.5 us (37%)
  Pallas kernels  3.73 us (11%)
  other arithmetic  1.27 us (4%)
  local copies, waits for them, and re-layouts  0.71 us (2%)
  between operations  0.69 us (2%)
    ppermute x9, waiting for transfers between devices, swap(): lax.ppermute(x, axis, [(i, i ^ bit) for i in range(lax.axis_size(axis))])  15 us
    ppermute x9, starting transfers between devices, swap(): lax.ppermute(x, axis, [(i, i ^ bit) for i in range(lax.axis_size(axis))])  12.5 us
    pallas_call x1, Pallas kernels, shards(): pl.pallas_call(functools.partial(gain_kernel, layout, weeks, per_owner),...  2.09 us
    pallas_call x1, Pallas kernels, shards(): pl.pallas_call(functools.partial(pack_kernel, owners), out_shape=(packed,...  1.63 us
    dynamic_slice x1, local copies, waits for them, and re-layouts, shards(): lax.dynamic_slice_in_dim(gain, lax.axis_index('period') * share, share, 2)  0.69 us
  transfers between devices with their start and end apart: 9, of which 9 were waited for; matrix products, arithmetic and copies ran while one was open for 4% of the time, Pallas kernels for 0%

profile of v2, /device:TPU:0, one launch (start us, length us, event | category | flops | bytes accessed | tf_op | source)
XLA Modules:
  0.0 33.8 jit_solution(9900294439391903972)
XLA Ops:
  0.6 1.6 %shard_map.85 = (bf16[56,256]{1,0:T(8,128)(2,1)S(1)}, bf16[56,256]{1,0:T(8,128)(2,1)S(1)}) custom-call(s32[64,256]{1,0:T(8,128)} %bitcast.13, s32[1,256]{1,0:T(1,128)} %bitcast.15, s32[1,256]{1,0:T(1,128)} %bitcast.16, s32[1,256]{1,0:T(1,128)} %bitcast.17, s32[16,32]{1,0:T(8,128)} %chosen_ref.1, bf16[32,256]{1,0:T(8,128)(2,1)} %bitcast.14), custom_call_target="tpu_custom_call" | custom-call | tf_op jit(solution)/shard_map/pallas_call | solution.py:212
  2.3 4.1 %collective-permute-start = (bf16[56,256]{1,0:T(8,128)(2,1)S(1)}, bf16[56,256]{1,0:T(8,128)(2,1)S(1)}, u32[]{:S(2)}, u32[]{:S(2)}) collective-permute-start(bf16[56,256]{1,0:T(8,128)(2,1)S(1)} %get-tuple-element.8), channel_id=1, source_target_pairs={{0,16},{4,20},{8,24},{12,28},{16,0},{20,4},{24,8},{28,12},{1,17},{... | collective-permute-start | bytes 86024 | tf_op jit(solution)/shard_map/ppermute | solution.py:208
  6.4 1.8 %collective-permute-done = bf16[56,256]{1,0:T(8,128)(2,1)S(1)} collective-permute-done((bf16[56,256]{1,0:T(8,128)(2,1)S(1)}, bf16[56,256]{1,0:T(8,128)(2,1)S(1)}, u32[]{:S(2)}, u32[]{:S(2)}) %collective-permute-start) | collective-permute-done | bytes 28704 | tf_op jit(solution)/shard_map/ppermute | solution.py:208
  8.3 2.9 %collective-permute-start.1 = (bf16[2,40,256]{2,1,0:T(8,128)(2,1)S(1)}, bf16[2,40,256]{2,1,0:T(8,128)(2,1)S(1)}, u32[]{:S(2)}, u32[]{:S(2)}) collective-permute-start(bf16[2,40,256]{2,1,0:T(8,128)(2,1)S(1)} %get-tuple-element.15), channel_id=1, source_target_pairs={{0,12},{4,8},{8,4},{12,0},{16,28},{20,24},{24,20},{28,16},{1,13},{... | collective-permute-start | bytes 122888 | tf_op jit(solution)/shard_map/ppermute | solution.py:208
  11.2 0.6 %collective-permute-start.2 = (bf16[2,40,256]{2,1,0:T(8,128)(2,1)S(1)}, bf16[2,40,256]{2,1,0:T(8,128)(2,1)S(1)}, u32[]{:S(2)}, u32[]{:S(2)}) collective-permute-start(bf16[2,40,256]{2,1,0:T(8,128)(2,1)S(1)} %get-tuple-element.14), channel_id=1, source_target_pairs={{0,8},{4,12},{8,0},{12,4},{16,24},{20,28},{24,16},{28,20},{1,9},{5... | collective-permute-start | bytes 122888 | tf_op jit(solution)/shard_map/ppermute | solution.py:208
  11.8 0.0 collective-permute-start.3
  11.8 1.4 %collective-permute-done.1.refs_2_ = bf16[2,40,256]{2,1,0:T(8,128)(2,1)S(1)} collective-permute-done((bf16[2,40,256]{2,1,0:T(8,128)(2,1)S(1)}, bf16[2,40,256]{2,1,0:T(8,128)(2,1)S(1)}, u32[]{:S(2)}, u32[]{:S(2)}) %collective-permute-start.1) | collective-permute-done | bytes 40992 | tf_op jit(solution)/shard_map/ppermute | solution.py:208
  13.2 1.9 %collective-permute-done.2.refs_3_ = bf16[2,40,256]{2,1,0:T(8,128)(2,1)S(1)} collective-permute-done((bf16[2,40,256]{2,1,0:T(8,128)(2,1)S(1)}, bf16[2,40,256]{2,1,0:T(8,128)(2,1)S(1)}, u32[]{:S(2)}, u32[]{:S(2)}) %collective-permute-start.2) | collective-permute-done | bytes 40992 | tf_op jit(solution)/shard_map/ppermute | solution.py:208
  15.2 0.6 %collective-permute-done.3.refs_4_ = bf16[2,40,256]{2,1,0:T(8,128)(2,1)S(1)} collective-permute-done((bf16[2,40,256]{2,1,0:T(8,128)(2,1)S(1)}, bf16[2,40,256]{2,1,0:T(8,128)(2,1)S(1)}, u32[]{:S(2)}, u32[]{:S(2)}) %collective-permute-start.3) | collective-permute-done | bytes 40992 | tf_op jit(solution)/shard_map/ppermute | solution.py:208
  15.8 2.1 %shard_map.86 = (f32[4,16,256]{2,1,0:T(8,128)S(1)}, f32[32,32]{1,0:T(8,128)S(1)}) custom-call(bf16[1,56,256]{2,1,0:T(8,128)(2,1)S(1)} %bitcast.9, bf16[1,56,256]{2,1,0:T(8,128)(2,1)S(1)} %bitcast.12, bf16[2,40,256]{2,1,0:T(8,128)(2,1)S(1)} %collective-permute-done.1.refs_2_, bf16[2,40,256]{2,1,0:T(8,128)(2,1)S(1)} %collective-permute-done.2.refs_3_, ...), custom_call_target="tpu_custom_call" | custom-call | tf_op jit(solution)/shard_map/pallas_call | solution.py:243
  17.9 0.1 collective-permute-start.4
  18.0 1.2 %collective-permute-done.4 = f32[4,16,256]{2,1,0:T(8,128)S(1)} collective-permute-done((f32[4,16,256]{2,1,0:T(8,128)S(1)}, f32[4,16,256]{2,1,0:T(8,128)S(1)}, u32[]{:S(2)}, u32[]{:S(2)}) %collective-permute-start.4) | collective-permute-done | bytes 65568 | tf_op jit(solution)/shard_map/ppermute | solution.py:208
  19.2 1.3 %collective-permute-start.5 = (f32[4,16,256]{2,1,0:T(8,128)S(1)}, f32[4,16,256]{2,1,0:T(8,128)S(1)}, u32[]{:S(2)}, u32[]{:S(2)}) collective-permute-start(f32[4,16,256]{2,1,0:T(8,128)S(1)} %add.9), channel_id=1, source_target_pairs={{0,3},{1,2},{2,1},{3,0},{4,7},{5,6},{6,5},{7,4},{8,11},{9,10},{10,... | collective-permute-start | bytes 196616 | tf_op jit(solution)/shard_map/ppermute | solution.py:208
  20.6 2.8 %collective-permute-done.5 = f32[4,16,256]{2,1,0:T(8,128)S(1)} collective-permute-done((f32[4,16,256]{2,1,0:T(8,128)S(1)}, f32[4,16,256]{2,1,0:T(8,128)S(1)}, u32[]{:S(2)}, u32[]{:S(2)}) %collective-permute-start.5) | collective-permute-done | bytes 65568 | tf_op jit(solution)/shard_map/ppermute | solution.py:208
  23.3 0.1 fusion.3
  23.5 0.1 collective-permute-start.6
  23.5 3.0 %collective-permute-done.6 = f32[16]{0:T(128)S(1)} collective-permute-done((f32[16]{0:T(128)S(1)}, f32[16]{0:T(128)S(1)}, u32[]{:S(2)}, u32[]{:S(2)}) %collective-permute-start.6) | collective-permute-done | bytes 96 | tf_op jit(solution)/shard_map/ppermute | solution.py:208
  26.5 1.2 %collective-permute-start.7 = (f32[16]{0:T(128)S(1)}, f32[16]{0:T(128)S(1)}, u32[]{:S(2)}, u32[]{:S(2)}) collective-permute-start(f32[16]{0:T(128)S(1)} %max.9), channel_id=1, source_target_pairs={{0,9},{1,8},{2,11},{3,10},{4,13},{5,12},{6,15},{7,14},{8,1},{9,0},... | collective-permute-start | bytes 200 | tf_op jit(solution)/shard_map/ppermute | solution.py:208
  27.7 0.6 %slice_subtract_fusion = f32[16,32]{1,0:T(8,128)} fusion(f32[32,32]{1,0:T(8,128)S(1)} %get-tuple-element.10), kind=kLoop, calls=%fused_computation.9 | loop fusion | flops 512 | bytes 6144 | tf_op jit(solution)/shard_map/sub | solution.py:268
  28.3 1.2 %collective-permute-done.7 = f32[16]{0:T(128)S(1)} collective-permute-done((f32[16]{0:T(128)S(1)}, f32[16]{0:T(128)S(1)}, u32[]{:S(2)}, u32[]{:S(2)}) %collective-permute-start.7) | collective-permute-done | bytes 96 | tf_op jit(solution)/shard_map/ppermute | solution.py:208
  29.5 2.2 %collective-permute-start.8 = (f32[16]{0:T(128)S(1)}, f32[16]{0:T(128)S(1)}, u32[]{:S(2)}, u32[]{:S(2)}) collective-permute-start(f32[16]{0:T(128)S(1)} %max.10), channel_id=1, source_target_pairs={{0,17},{1,16},{2,19},{3,18},{4,21},{5,20},{6,23},{7,22},{8,25},{9,... | collective-permute-start | bytes 200 | tf_op jit(solution)/shard_map/ppermute | solution.py:208
  31.7 0.7 %constant_dynamic-slice_fusion = f32[4,16,64]{2,1,0:T(8,128)} fusion(f32[4,16,256]{2,1,0:T(8,128)S(1)} %get-tuple-element.12, s32[]{:T(128)S(6)} %select_n.3), kind=kLoop, calls=%fused_computation.10 | loop fusion | bytes 32772 | tf_op jit(solution)/shard_map/dynamic_slice | solution.py:262
  32.4 1.0 %collective-permute-done.8 = f32[16]{0:T(128)S(1)} collective-permute-done((f32[16]{0:T(128)S(1)}, f32[16]{0:T(128)S(1)}, u32[]{:S(2)}, u32[]{:S(2)}) %collective-permute-start.8) | collective-permute-done | bytes 96 | tf_op jit(solution)/shard_map/ppermute | solution.py:208
  33.3 0.5 %max.11 = f32[16]{0:T(128)} maximum(f32[16]{0:T(128)S(1)} %max.10, f32[16]{0:T(128)S(1)} %collective-permute-done.8) | non-fusion elementwise | flops 16 | bytes 192 | tf_op jit(solution)/shard_map/max | solution.py:266
  (8 shorter events, 0.1 us)
Async XLA Ops:
  2.3 6.0 %collective-permute-start = (bf16[56,256]{1,0:T(8,128)(2,1)S(1)}, bf16[56,256]{1,0:T(8,128)(2,1)S(1)}, u32[]{:S(2)}, u32[]{:S(2)}) collective-permute-start(bf16[56,256]{1,0:T(8,128)(2,1)S(1)} %get-tuple-element.8), channel_id=1, source_target_pairs={{0,16},{4,20},{8,24},{12,28},{16,0},{20,4},{24,8},{28,12},{1,17},{... | collective-permute-start | bytes 86024 | tf_op jit(solution)/shard_map/ppermute | solution.py:208
  8.3 5.0 %collective-permute-start.1 = (bf16[2,40,256]{2,1,0:T(8,128)(2,1)S(1)}, bf16[2,40,256]{2,1,0:T(8,128)(2,1)S(1)}, u32[]{:S(2)}, u32[]{:S(2)}) collective-permute-start(bf16[2,40,256]{2,1,0:T(8,128)(2,1)S(1)} %get-tuple-element.15), channel_id=1, source_target_pairs={{0,12},{4,8},{8,4},{12,0},{16,28},{20,24},{24,20},{28,16},{1,13},{... | collective-permute-start | bytes 122888 | tf_op jit(solution)/shard_map/ppermute | solution.py:208
  11.2 4.0 %collective-permute-start.2 = (bf16[2,40,256]{2,1,0:T(8,128)(2,1)S(1)}, bf16[2,40,256]{2,1,0:T(8,128)(2,1)S(1)}, u32[]{:S(2)}, u32[]{:S(2)}) collective-permute-start(bf16[2,40,256]{2,1,0:T(8,128)(2,1)S(1)} %get-tuple-element.14), channel_id=1, source_target_pairs={{0,8},{4,12},{8,0},{12,4},{16,24},{20,28},{24,16},{28,20},{1,9},{5... | collective-permute-start | bytes 122888 | tf_op jit(solution)/shard_map/ppermute | solution.py:208
  11.8 4.0 %collective-permute-start.3 = (bf16[2,40,256]{2,1,0:T(8,128)(2,1)S(1)}, bf16[2,40,256]{2,1,0:T(8,128)(2,1)S(1)}, u32[]{:S(2)}, u32[]{:S(2)}) collective-permute-start(bf16[2,40,256]{2,1,0:T(8,128)(2,1)S(1)} %get-tuple-element.13), channel_id=1, source_target_pairs={{0,4},{4,0},{8,12},{12,8},{16,20},{20,16},{24,28},{28,24},{1,5},{5... | collective-permute-start | bytes 122888 | tf_op jit(solution)/shard_map/ppermute | solution.py:208
  17.9 1.3 %collective-permute-start.4 = (f32[4,16,256]{2,1,0:T(8,128)S(1)}, f32[4,16,256]{2,1,0:T(8,128)S(1)}, u32[]{:S(2)}, u32[]{:S(2)}) collective-permute-start(f32[4,16,256]{2,1,0:T(8,128)S(1)} %get-tuple-element.9), channel_id=1, source_target_pairs={{0,1},{1,0},{2,3},{3,2},{4,5},{5,4},{6,7},{7,6},{8,9},{9,8},{10,11... | collective-permute-start | bytes 196616 | tf_op jit(solution)/shard_map/ppermute | solution.py:208
  19.2 4.1 %collective-permute-start.5 = (f32[4,16,256]{2,1,0:T(8,128)S(1)}, f32[4,16,256]{2,1,0:T(8,128)S(1)}, u32[]{:S(2)}, u32[]{:S(2)}) collective-permute-start(f32[4,16,256]{2,1,0:T(8,128)S(1)} %add.9), channel_id=1, source_target_pairs={{0,3},{1,2},{2,1},{3,0},{4,7},{5,6},{6,5},{7,4},{8,11},{9,10},{10,... | collective-permute-start | bytes 196616 | tf_op jit(solution)/shard_map/ppermute | solution.py:208
  23.5 3.0 %collective-permute-start.6 = (f32[16]{0:T(128)S(1)}, f32[16]{0:T(128)S(1)}, u32[]{:S(2)}, u32[]{:S(2)}) collective-permute-start(f32[16]{0:T(128)S(1)} %get-tuple-element.11), channel_id=1, source_target_pairs={{0,5},{1,4},{2,7},{3,6},{4,1},{5,0},{6,3},{7,2},{8,13},{9,12},{10,... | collective-permute-start | bytes 200 | tf_op jit(solution)/shard_map/ppermute | solution.py:208
  26.5 3.0 %collective-permute-start.7 = (f32[16]{0:T(128)S(1)}, f32[16]{0:T(128)S(1)}, u32[]{:S(2)}, u32[]{:S(2)}) collective-permute-start(f32[16]{0:T(128)S(1)} %max.9), channel_id=1, source_target_pairs={{0,9},{1,8},{2,11},{3,10},{4,13},{5,12},{6,15},{7,14},{8,1},{9,0},... | collective-permute-start | bytes 200 | tf_op jit(solution)/shard_map/ppermute | solution.py:208
  29.5 3.9 %collective-permute-start.8 = (f32[16]{0:T(128)S(1)}, f32[16]{0:T(128)S(1)}, u32[]{:S(2)}, u32[]{:S(2)}) collective-permute-start(f32[16]{0:T(128)S(1)} %max.10), channel_id=1, source_target_pairs={{0,17},{1,16},{2,19},{3,18},{4,21},{5,20},{6,23},{7,22},{8,25},{9,... | collective-permute-start | bytes 200 | tf_op jit(solution)/shard_map/ppermute | solution.py:208

commit v3 on v2

v3 whole, which is shorter than its diff:
```python
import functools

import jax
import jax.numpy as jnp
from jax import lax
from jax.experimental import pallas as pl
from jax.experimental.pallas import tpu as pltpu
from jax.sharding import PartitionSpec as P

NODES = 16
BINS = 256
LANES = 128
PAIRS = NODES // 2
BF16 = jnp.bfloat16
F32 = jnp.float32
NT = (((1,), (1,)), ((), ()))


def iota(shape, axis):
    return lax.broadcasted_iota(jnp.int32, shape, axis)


def dot(a, b, dims=(((1,), (0,)), ((), ()))):
    return lax.dot_general(a.astype(BF16), b.astype(BF16), dims, preferred_element_type=F32)


def place_kernel(owners, codes_ref, node_ref, arm_ref, honest_ref, chosen_ref, outcome_ref, place_ref, mine_ref, scratch):
    covars, units = codes_ref.shape
    slots, weeks = chosen_ref.shape[1], outcome_ref.shape[0]
    per_owner = slots // owners
    room = units // PAIRS
    me = lax.axis_index("row")
    node, arm, honest = node_ref[...], arm_ref[...], honest_ref[...]

    before = (iota((units, units), 0) < iota((units, units), 1)).astype(BF16)
    pair = lax.shift_right_logical(node, 1)
    group = iota((PAIRS, units), 0)
    in_pair = ((group == pair) & (honest == 1)).astype(F32)
    earlier = dot(in_pair, before)
    index = jnp.sum(in_pair * earlier, axis=0, keepdims=True)
    placed = (honest == 1) & (index < room)
    placed_earlier = jnp.sum(jnp.minimum(earlier, float(room)), axis=0, keepdims=True)
    filler_rank = iota((1, units), 1).astype(F32) - placed_earlier
    held = jnp.minimum(jnp.sum(in_pair, axis=1, keepdims=True), float(room))
    free = jnp.broadcast_to(room - held, (PAIRS, units))
    first = free
    for step in (1, 2, 4):
        first = first + jnp.concatenate([jnp.zeros((step, units), F32), first[: PAIRS - step]], axis=0)
    first = first - free
    in_gap = (filler_rank >= first) & (filler_rank < first + free)
    gap_lane = jnp.sum(
        jnp.where(in_gap, group.astype(F32) * room + held - first + filler_rank, 0.0), axis=0, keepdims=True
    )
    lane = jnp.where(placed, pair * room + index.astype(jnp.int32), gap_lane.astype(jnp.int32))
    lane = lane ^ (room * (me & 3))
    place = jnp.where(iota((units, units), 0) == lane, 1.0, 0.0).astype(BF16)
    place_ref[...] = place

    flat = jnp.concatenate([chosen_ref[n : n + 1, :] for n in range(NODES)], axis=1)
    hot = jnp.where(iota((covars, NODES * slots), 0) == flat, 1.0, 0.0)
    per_node = dot(hot, codes_ref[...].astype(F32), (((0,), (0,)), ((), ())))
    picked = jnp.zeros((slots, units), F32)
    for n in range(NODES):
        picked = picked + jnp.where(node == n, per_node[n * slots : (n + 1) * slots], 0.0)
    for j in range(owners):
        scratch[j, 0:per_owner] = picked[j * per_owner : (j + 1) * per_owner]
    ordered = [scratch[me ^ j ^ k][0:per_owner] for j in range(owners // 2) for k in (0, owners // 2)]

    keys = [node.astype(F32), arm.astype(F32), honest.astype(F32), jnp.zeros((1, units), F32)]
    wide = jnp.concatenate([outcome_ref[...].astype(F32), *keys, *ordered, jnp.zeros((4, units), F32)], axis=0)
    mine_ref[...] = dot(wide, place, NT)


def join_kernel(per_owner, place_ref, mine_ref, other_ref, own_ref, away_ref):
    weeks = other_ref.shape[0]
    mine = mine_ref[...]
    tail = mine[weeks:]
    outcome, other = mine[0:weeks], dot(other_ref[...], place_ref[...], NT)
    first = (lax.axis_index("period") & 1) == 0
    both = [jnp.where(first, outcome, other), jnp.where(first, other, outcome)]
    own_ref[...] = jnp.concatenate([*both, tail], axis=0).astype(BF16)
    turned = [
        tail[at : at + per_owner]
        for pair in range(4, tail.shape[0] - 4, 2 * per_owner)
        for at in (pair + per_owner, pair)
    ]
    away_ref[...] = jnp.concatenate([*both, tail[0:4], *turned, tail[-4:]], axis=0).astype(BF16)


def gain_kernel(layout, per_owner, periods, *refs):
    n_in = len(layout)
    blocks = refs[:n_in]
    gain_ref, effect_ref, outs, keys, sums = refs[n_in:]
    weeks, depth, key_rows = outs.shape[1], outs.shape[2], keys.shape[1]
    me, period = lax.axis_index("row"), lax.axis_index("period")
    where_of = {k: (ref, at) for ref, ids in zip(blocks, layout) for at, k in enumerate(ids)}
    n_blocks = len(where_of)
    quarter = lax.shift_right_logical(iota((8, LANES), 1), 5) ^ (me & 3)
    masks = [quarter == t for t in range(4)]
    one, zero = jnp.ones((), BF16), jnp.zeros((), BF16)

    share = BINS // periods
    row = iota((BINS // 2, depth), 0)
    index, within = row // share, row % share
    odd = period ^ index
    for shift in (2, 1):
        odd = odd ^ lax.shift_right_logical(odd, shift)
    bins_up = ((2 * index + (odd & 1)) * share + within + 1).astype(F32).astype(BF16)

    def loaded(k, half):
        ref, at = where_of[k]
        return ref[at, 0 : weeks + key_rows, half * LANES : (half + 1) * LANES].astype(F32)

    def week_rows(g, out, key):
        node, arm, honest = key[0:1], key[1:2], key[2:3]
        mine, counts = [], []
        for m in range(2):
            of_node = (node == (2 * g + m).astype(F32)) & (honest == 1.0)
            for a in (1.0, 0.0):
                here = jnp.where(of_node & (arm == a), 1.0, 0.0)
                mine.append(out * here)
                counts.append(jnp.broadcast_to(here, (8, here.shape[1])))
        return jnp.concatenate(mine + counts, axis=0)

    def step_rows(key, tile):
        steps = []
        for s in (2 * tile, 2 * tile + 1):
            pick = jnp.broadcast_to(key[4 + s : 5 + s], (16, key.shape[1])).astype(BF16)
            pick = jnp.concatenate([pick] * (BINS // 32), axis=0)
            steps.append(jnp.maximum(jnp.minimum(bins_up - pick, one), zero))
        return jnp.concatenate(steps, axis=0)

    def pair_gains(left, total):
        gains = []
        for m in range(2):
            base, count = 2 * m * weeks, 4 * weeks + 16 * m
            treated, control = left[base : base + weeks], left[base + weeks : base + 2 * weeks]
            all_treated, all_control = total[base : base + weeks], total[base + weeks : base + 2 * weeks]
            lt, lc = left[count : count + 8], left[count + 8 : count + 16]
            rt, rc = total[count : count + 8] - lt, total[count + 8 : count + 16] - lc
            it, ic = 1.0 / (rt + 1.0), 1.0 / (rc + 1.0)
            at, ac = 1.0 / (lt + 1.0) + it, 1.0 / (lc + 1.0) + ic
            spread = None
            for w in range(0, weeks, 8):
                rng = slice(w, w + 8)
                gap = (treated[rng] * at - all_treated[rng] * it) - (control[rng] * ac - all_control[rng] * ic)
                spread = gap * gap if spread is None else spread + gap * gap
            cl, cr = lt + lc, rt + rc
            balance = cl * cr / ((cl + cr + 1.0) * (cl + cr + 1.0))
            gains.append(jnp.sum(balance * spread, axis=0, keepdims=True))
        return gains

    def totals(mine):
        return jnp.broadcast_to(jnp.sum(mine, axis=1, keepdims=True), (mine.shape[0], BINS))

    def store(tile, rows, gain):
        gain_ref[2 * tile, rows] = gain[:, : BINS // 2]
        gain_ref[2 * tile + 1, rows] = gain[:, BINS // 2 :]

    strays = jnp.zeros((1, depth), F32)
    est = jnp.zeros((2 * NODES, weeks // 2), F32)
    est_units = jnp.zeros((2 * NODES, depth), F32)
    for half in range(2):
        held = [loaded(k, half) for k in range(n_blocks)]
        for g in range(half * 4, half * 4 + 4):
            parts = []
            for first in range(0, n_blocks, 4):
                part = held[first]
                for k in range(first + 1, first + 4):
                    mask = jnp.concatenate([masks[(g ^ k) & 3]] * (part.shape[0] // 8), axis=0)
                    part = jnp.where(mask, held[k], part)
                parts.append(part)
            block = jnp.concatenate(parts, axis=1)
            out, key = block[0:weeks], block[weeks:]
            outs[g] = out
            keys[g] = key
            node, arm, honest = key[0:1], key[1:2], key[2:3]
            strays = strays + jnp.where((honest == 1.0) & ((node < 2.0 * g) | (node > 2.0 * g + 1.0)), 1.0, 0.0)
            kept = jnp.where(honest == 0.0, node, -1.0)
            kept_hot = kept == iota((NODES, depth), 0).astype(F32)
            hot = jnp.concatenate(
                [jnp.where(kept_hot & (arm == a), 1.0, 0.0) for a in (1.0, 0.0)], axis=0
            )
            est = est + dot(hot, jnp.where((period & 1) == 0, out[: weeks // 2], out[weeks // 2 :]), NT)
            est_units = est_units + hot
            mine = week_rows(jnp.int32(g), out, key)
            total = totals(mine)
            for tile in range(per_owner):
                left = dot(mine, step_rows(key, tile), NT)
                for m, gain in enumerate(pair_gains(left, total)):
                    store(tile, slice(2 * g + m, 2 * g + m + 1), gain)

    units = jnp.sum(est_units, axis=1, keepdims=True)
    effect_ref[...] = est / (units + 1.0)

    @pl.when(jnp.sum(strays) > 0.0)
    def _():
        def over_pairs(g, carry):
            for tile in range(per_owner):
                sums[...] = jnp.zeros_like(sums)

                def over_lanes(other, total):
                    mine = week_rows(g, outs[other], keys[other])
                    sums[...] += dot(mine, step_rows(keys[other], tile), NT)
                    return total + totals(mine)

                total = lax.fori_loop(0, PAIRS, over_lanes, jnp.zeros(sums.shape, F32))
                for m, gain in enumerate(pair_gains(sums[...], total)):
                    store(tile, pl.ds(2 * g + m, 1), gain)
            return carry

        lax.fori_loop(0, PAIRS, over_pairs, 0)


def shards(codes, node, chosen, arm, honest, outcome):
    units, weeks = outcome.shape
    slots = chosen.shape[1]
    owners, periods = lax.axis_size("row"), lax.axis_size("period")
    per_owner = slots // owners
    vmem = pl.BlockSpec(memory_space=pltpu.VMEM)

    def swap(x, axis, bit):
        return lax.ppermute(x, axis, [(i, i ^ bit) for i in range(lax.axis_size(axis))])

    def cross(x, bit):
        return swap(x, ("row", "period"), bit * periods | 1)

    inputs = (codes.T, node.reshape(1, units), arm.reshape(1, units), honest.reshape(1, units), chosen, outcome.T)
    other = swap(outcome.T, "period", 1)
    place, mine = pl.pallas_call(
        functools.partial(place_kernel, owners),
        out_shape=(
            jax.ShapeDtypeStruct((units, units), BF16),
            jax.ShapeDtypeStruct((weeks + 8 + slots, units), F32),
        ),
        in_specs=[vmem] * 6,
        out_specs=(vmem, vmem),
        compiler_params=pltpu.CompilerParams(vmem_limit_bytes=8 * 1024 * 1024),
        scratch_shapes=[pltpu.VMEM((owners, -(-per_owner // 8) * 8, units), F32)],
    )(*(pltpu.with_memory_space_constraint(x, pltpu.HBM) for x in inputs))
    packed = jax.ShapeDtypeStruct((2 * weeks + 8 + slots, units), BF16)
    own, away = pl.pallas_call(
        functools.partial(join_kernel, per_owner),
        out_shape=(packed, packed),
        in_specs=[vmem] * 3,
        out_specs=(vmem, vmem),
        compiler_params=pltpu.CompilerParams(vmem_limit_bytes=4 * 1024 * 1024),
    )(place, mine, other)

    bins_at, width = 2 * weeks + 4, 2 * per_owner
    key_rows = -(-(4 + width) // 8) * 8

    def part(x, first, last, more):
        return jnp.concatenate([x[:, :bins_at], x[:, bins_at + first * width : bins_at + last * width + more]], axis=1)

    half = owners // 2
    held = [(own[None], [0]), (cross(away, half)[None], [half])]
    groups = half
    while groups > 4:
        groups //= 2
        ids = [k for _, some in held for k in some]
        whole = jnp.concatenate([x for x, _ in held], axis=0)
        came = cross(part(whole, groups, 2 * groups, 4), groups)
        held = [(part(whole, 0, groups, 4), ids), (came, [k ^ groups for k in ids])]
    ids = [k for _, some in held for k in some]
    layout = [some for _, some in held]
    blocks = [x for x, _ in held]
    for k in (3, 2, 1):
        send = jnp.concatenate([part(x, k, k + 1, key_rows - 4 - width) for x, _ in held], axis=0)
        blocks.append(cross(send, k))
        layout.append([i ^ k for i in ids])

    depth = owners * units // PAIRS
    gain, effect = pl.pallas_call(
        functools.partial(gain_kernel, layout, per_owner, periods),
        out_shape=(
            jax.ShapeDtypeStruct((2 * per_owner, NODES, BINS // 2), F32),
            jax.ShapeDtypeStruct((2 * NODES, weeks), F32),
        ),
        in_specs=[vmem] * len(blocks),
        out_specs=(vmem, vmem),
        scratch_shapes=[
            pltpu.VMEM((PAIRS, 2 * weeks, depth), F32),
            pltpu.VMEM((PAIRS, key_rows, depth), F32),
            pltpu.VMEM((8 * weeks + 32, BINS), F32),
        ],
        compiler_params=pltpu.CompilerParams(vmem_limit_bytes=16 * 1024 * 1024),
    )(*blocks)

    bit = 2
    while bit < periods:
        gain = gain + swap(gain, "period", bit | 1)
        bit *= 2
    share = BINS // periods
    gains = lax.dynamic_slice_in_dim(gain[:per_owner], (lax.axis_index("period") >> 1) * share, share, 2)
    best = jnp.max(gain, axis=(0, 2))
    best = jnp.maximum(best, swap(best, "period", 1))
    bit = 1
    while bit < half:
        best = jnp.maximum(best, cross(best, bit))
        bit *= 2
    return gains, best, effect[:NODES] - effect[NODES:]


def solution(mesh):
    in_specs = (P("row", None), P("row"), P(), P("row"), P("row"), P("row", "period"))
    out_specs = (P("row", None, "period"), P(), P(None, "period"))
    return jax.shard_map(shards, mesh=mesh, in_specs=in_specs, out_specs=out_specs, check_vma=False)
```

time: 34 us -> 31.2 us (0.918)
  waiting for transfers between devices: 15 us -> 9.57 us
  starting transfers between devices: 12.5 us -> 14.4 us
  Pallas kernels: 3.73 us -> 4.44 us
    ppermute x9, waiting for transfers between devices: 15 us -> 9.57 us  [swap(): lax.ppermute(x, axis, [(i, i ^ bit) for i in range(lax.axis_size(axis))])]
    ppermute x9, starting transfers between devices: 12.5 us -> 14.4 us  [swap(): lax.ppermute(x, axis, [(i, i ^ bit) for i in range(lax.axis_size(axis))])]
    pallas_call x2 -> x3, Pallas kernels: 3.73 us -> 4.44 us  [the longest x1 2.89 us: shards(): pl.pallas_call(functools.partial(gain_kernel, layout, per_owner, periods)...]
  transfers between devices with their start and end apart: 9 -> 9, of which waited for: 9 -> 7; matrix products, arithmetic and copies ran while one was open for 4% -> 4% of each run, Pallas kernels for 0% -> 4%
where the time goes in v3:
time: 31.2 us; the launch traced here: 31.1 us
  starting transfers between devices  14.4 us (46%)
  waiting for transfers between devices  9.57 us (31%)
  Pallas kernels  4.44 us (14%)
  other arithmetic  1.27 us (4%)
  local copies, waits for them, and re-layouts  0.72 us (2%)
  between operations  0.69 us (2%)
    ppermute x9, starting transfers between devices, swap(): lax.ppermute(x, axis, [(i, i ^ bit) for i in range(lax.axis_size(axis))])  14.4 us
    ppermute x9, waiting for transfers between devices, swap(): lax.ppermute(x, axis, [(i, i ^ bit) for i in range(lax.axis_size(axis))])  9.57 us
    pallas_call x1, Pallas kernels, shards(): pl.pallas_call(functools.partial(gain_kernel, layout, per_owner, periods)...  2.89 us
    pallas_call x1, Pallas kernels, shards(): pl.pallas_call(functools.partial(place_kernel, owners), out_shape=(jax.Sh...  1.39 us
    dynamic_slice x1, local copies, waits for them, and re-layouts, shards(): lax.dynamic_slice_in_dim(gain[:per_owner], (lax.axis_index('period') >> 1...  0.69 us
  transfers between devices with their start and end apart: 9, of which 7 were waited for; matrix products, arithmetic and copies ran while one was open for 4% of the time, Pallas kernels for 4%

profile of v3, /device:TPU:0, one launch (start us, length us, event | category | flops | bytes accessed | tf_op | source)
XLA Modules:
  0.0 31.1 jit_solution(4271604037601942421)
XLA Ops:
  0.6 0.5 %collective-permute-start = (bf16[32,256]{1,0:T(8,128)(2,1)}, bf16[32,256]{1,0:T(8,128)(2,1)S(1)}, u32[]{:S(2)}, u32[]{:S(2)}) collective-permute-start(bf16[32,256]{1,0:T(8,128)(2,1)} %bitcast.14), channel_id=1, source_target_pairs={{0,1},{1,0},{2,3},{3,2},{4,5},{5,4},{6,7},{7,6},{8,9},{9,8},{10,11... | collective-permute-start | bytes 49160 | tf_op jit(solution)/shard_map/ppermute | solution.py:223
  1.1 1.4 %shard_map.85 = (bf16[256,256]{1,0:T(8,128)(2,1)S(1)}, f32[72,256]{1,0:T(8,128)S(1)}) custom-call(s32[64,256]{1,0:T(8,128)} %bitcast.13, s32[1,256]{1,0:T(1,128)} %bitcast.16, s32[1,256]{1,0:T(1,128)} %bitcast.17, s32[1,256]{1,0:T(1,128)} %bitcast.18, s32[16,32]{1,0:T(8,128)} %chosen_ref.1, bf16[32,256]{1,0:T(8,128)(2,1)} %bitcast.15), custom_call_target="tpu_custom_call" | custom-call | tf_op jit(solution)/shard_map/pallas_call | solution.py:230
  2.5 0.0 collective-permute-done.other_ref
  2.6 0.2 shard_map.86
  2.7 3.7 %collective-permute-start.1 = (bf16[104,256]{1,0:T(8,128)(2,1)S(1)}, bf16[104,256]{1,0:T(8,128)(2,1)S(1)}, u32[]{:S(2)}, u32[]{:S(2)}) collective-permute-start(bf16[104,256]{1,0:T(8,128)(2,1)S(1)} %get-tuple-element.12), channel_id=1, source_target_pairs={{0,17},{1,16},{2,19},{3,18},{4,21},{5,20},{6,23},{7,22},{8,25},{9,... | collective-permute-start | bytes 159752 | tf_op jit(solution)/shard_map/ppermute | solution.py:223
  6.5 2.2 %collective-permute-done.1 = bf16[104,256]{1,0:T(8,128)(2,1)S(1)} collective-permute-done((bf16[104,256]{1,0:T(8,128)(2,1)S(1)}, bf16[104,256]{1,0:T(8,128)(2,1)S(1)}, u32[]{:S(2)}, u32[]{:S(2)}) %collective-permute-start.1) | collective-permute-done | bytes 53280 | tf_op jit(solution)/shard_map/ppermute | solution.py:223
  8.7 2.6 %collective-permute-start.2 = (bf16[2,80,256]{2,1,0:T(8,128)(2,1)S(1)}, bf16[2,80,256]{2,1,0:T(8,128)(2,1)S(1)}, u32[]{:S(2)}, u32[]{:S(2)}) collective-permute-start(bf16[2,80,256]{2,1,0:T(8,128)(2,1)S(1)} %get-tuple-element.19), channel_id=1, source_target_pairs={{0,13},{1,12},{2,15},{3,14},{4,9},{5,8},{6,11},{7,10},{8,5},{9,4},... | collective-permute-start | bytes 245768 | tf_op jit(solution)/shard_map/ppermute | solution.py:223
  11.2 0.0 collective-permute-start.3
  11.3 1.5 %collective-permute-start.4 = (bf16[2,80,256]{2,1,0:T(8,128)(2,1)S(1)}, bf16[2,80,256]{2,1,0:T(8,128)(2,1)S(1)}, u32[]{:S(2)}, u32[]{:S(2)}) collective-permute-start(bf16[2,80,256]{2,1,0:T(8,128)(2,1)S(1)} %get-tuple-element.17), channel_id=1, source_target_pairs={{0,5},{1,4},{2,7},{3,6},{4,1},{5,0},{6,3},{7,2},{8,13},{9,12},{10,... | collective-permute-start | bytes 245768 | tf_op jit(solution)/shard_map/ppermute | solution.py:223
  12.7 1.4 %collective-permute-done.2.refs_2_ = bf16[2,80,256]{2,1,0:T(8,128)(2,1)S(1)} collective-permute-done((bf16[2,80,256]{2,1,0:T(8,128)(2,1)S(1)}, bf16[2,80,256]{2,1,0:T(8,128)(2,1)S(1)}, u32[]{:S(2)}, u32[]{:S(2)}) %collective-permute-start.2) | collective-permute-done | bytes 81952 | tf_op jit(solution)/shard_map/ppermute | solution.py:223
  14.1 1.9 %collective-permute-done.3.refs_3_ = bf16[2,80,256]{2,1,0:T(8,128)(2,1)S(1)} collective-permute-done((bf16[2,80,256]{2,1,0:T(8,128)(2,1)S(1)}, bf16[2,80,256]{2,1,0:T(8,128)(2,1)S(1)}, u32[]{:S(2)}, u32[]{:S(2)}) %collective-permute-start.3) | collective-permute-done | bytes 81952 | tf_op jit(solution)/shard_map/ppermute | solution.py:223
  16.0 0.0 collective-permute-done.4.refs_4_
  16.0 2.9 %shard_map.87 = (f32[8,16,128]{2,1,0:T(8,128)S(1)}, f32[32,32]{1,0:T(8,128)S(1)}) custom-call(bf16[1,104,256]{2,1,0:T(8,128)(2,1)S(1)} %bitcast.9, bf16[1,104,256]{2,1,0:T(8,128)(2,1)S(1)} %bitcast.12, bf16[2,80,256]{2,1,0:T(8,128)(2,1)S(1)} %collective-permute-done.2.refs_2_, bf16[2,80,256]{2,1,0:T(8,128)(2,1)S(1)} %collective-permute-done.3.refs_3_, ...), custom_call_target="tpu_custom_call" | custom-call | tf_op jit(solution)/shard_map/pallas_call | solution.py:274
  18.9 1.7 %collective-permute-start.5 = (f32[8,16,128]{2,1,0:T(8,128)S(1)}, f32[8,16,128]{2,1,0:T(8,128)S(1)}, u32[]{:S(2)}, u32[]{:S(2)}) collective-permute-start(f32[8,16,128]{2,1,0:T(8,128)S(1)} %get-tuple-element.13), channel_id=1, source_target_pairs={{0,3},{1,2},{2,1},{3,0},{4,7},{5,6},{6,5},{7,4},{8,11},{9,10},{10,... | collective-permute-start | bytes 196616 | tf_op jit(solution)/shard_map/ppermute | solution.py:223
  20.6 2.0 %collective-permute-done.5 = f32[8,16,128]{2,1,0:T(8,128)S(1)} collective-permute-done((f32[8,16,128]{2,1,0:T(8,128)S(1)}, f32[8,16,128]{2,1,0:T(8,128)S(1)}, u32[]{:S(2)}, u32[]{:S(2)}) %collective-permute-start.5) | collective-permute-done | bytes 65568 | tf_op jit(solution)/shard_map/ppermute | solution.py:223
  22.7 0.1 fusion.3
  22.8 0.6 %collective-permute-start.6 = (f32[16]{0:T(128)S(1)}, f32[16]{0:T(128)S(1)}, u32[]{:S(2)}, u32[]{:S(2)}) collective-permute-start(f32[16]{0:T(128)S(1)} %get-tuple-element.15), channel_id=1, source_target_pairs={{0,1},{1,0},{2,3},{3,2},{4,5},{5,4},{6,7},{7,6},{8,9},{9,8},{10,11... | collective-permute-start | bytes 200 | tf_op jit(solution)/shard_map/ppermute | solution.py:223
  23.4 0.6 %slice_subtract_fusion = f32[16,32]{1,0:T(8,128)} fusion(f32[32,32]{1,0:T(8,128)S(1)} %get-tuple-element.14), kind=kLoop, calls=%fused_computation.9 | loop fusion | flops 512 | bytes 6144 | tf_op jit(solution)/shard_map/sub | solution.py:302
  24.0 0.2 collective-permute-done.6
  24.2 1.8 %collective-permute-start.7 = (f32[16]{0:T(128)S(1)}, f32[16]{0:T(128)S(1)}, u32[]{:S(2)}, u32[]{:S(2)}) collective-permute-start(f32[16]{0:T(128)S(1)} %max.9), channel_id=1, source_target_pairs={{0,5},{1,4},{2,7},{3,6},{4,1},{5,0},{6,3},{7,2},{8,13},{9,12},{10,... | collective-permute-start | bytes 200 | tf_op jit(solution)/shard_map/ppermute | solution.py:223
  26.0 1.3 %collective-permute-done.7 = f32[16]{0:T(128)S(1)} collective-permute-done((f32[16]{0:T(128)S(1)}, f32[16]{0:T(128)S(1)}, u32[]{:S(2)}, u32[]{:S(2)}) %collective-permute-start.7) | collective-permute-done | bytes 96 | tf_op jit(solution)/shard_map/ppermute | solution.py:223
  27.3 2.0 %collective-permute-start.8 = (f32[16]{0:T(128)S(1)}, f32[16]{0:T(128)S(1)}, u32[]{:S(2)}, u32[]{:S(2)}) collective-permute-start(f32[16]{0:T(128)S(1)} %max.10), channel_id=1, source_target_pairs={{0,9},{1,8},{2,11},{3,10},{4,13},{5,12},{6,15},{7,14},{8,1},{9,0},... | collective-permute-start | bytes 200 | tf_op jit(solution)/shard_map/ppermute | solution.py:223
  29.3 0.7 %constant_dynamic-slice_fusion = f32[4,16,64]{2,1,0:T(8,128)} fusion(f32[4,16,128]{2,1,0:T(8,128)S(1)} %slice.56, s32[]{:T(128)S(6)} %select_n.3), kind=kLoop, calls=%fused_computation.10 | loop fusion | bytes 32772 | tf_op jit(solution)/shard_map/dynamic_slice | solution.py:295
  30.0 0.6 %collective-permute-done.8 = f32[16]{0:T(128)S(1)} collective-permute-done((f32[16]{0:T(128)S(1)}, f32[16]{0:T(128)S(1)}, u32[]{:S(2)}, u32[]{:S(2)}) %collective-permute-start.8) | collective-permute-done | bytes 96 | tf_op jit(solution)/shard_map/ppermute | solution.py:223
  30.6 0.5 %max.11 = f32[16]{0:T(128)} maximum(f32[16]{0:T(128)S(1)} %max.10, f32[16]{0:T(128)S(1)} %collective-permute-done.8) | non-fusion elementwise | flops 16 | bytes 192 | tf_op jit(solution)/shard_map/max | solution.py:300
  (8 shorter events, 0.1 us)
Async XLA Ops:
  0.6 1.9 %collective-permute-start = (bf16[32,256]{1,0:T(8,128)(2,1)}, bf16[32,256]{1,0:T(8,128)(2,1)S(1)}, u32[]{:S(2)}, u32[]{:S(2)}) collective-permute-start(bf16[32,256]{1,0:T(8,128)(2,1)} %bitcast.14), channel_id=1, source_target_pairs={{0,1},{1,0},{2,3},{3,2},{4,5},{5,4},{6,7},{7,6},{8,9},{9,8},{10,11... | collective-permute-start | bytes 49160 | tf_op jit(solution)/shard_map/ppermute | solution.py:223
  2.7 5.9 %collective-permute-start.1 = (bf16[104,256]{1,0:T(8,128)(2,1)S(1)}, bf16[104,256]{1,0:T(8,128)(2,1)S(1)}, u32[]{:S(2)}, u32[]{:S(2)}) collective-permute-start(bf16[104,256]{1,0:T(8,128)(2,1)S(1)} %get-tuple-element.12), channel_id=1, source_target_pairs={{0,17},{1,16},{2,19},{3,18},{4,21},{5,20},{6,23},{7,22},{8,25},{9,... | collective-permute-start | bytes 159752 | tf_op jit(solution)/shard_map/ppermute | solution.py:223
  8.7 5.4 %collective-permute-start.2 = (bf16[2,80,256]{2,1,0:T(8,128)(2,1)S(1)}, bf16[2,80,256]{2,1,0:T(8,128)(2,1)S(1)}, u32[]{:S(2)}, u32[]{:S(2)}) collective-permute-start(bf16[2,80,256]{2,1,0:T(8,128)(2,1)S(1)} %get-tuple-element.19), channel_id=1, source_target_pairs={{0,13},{1,12},{2,15},{3,14},{4,9},{5,8},{6,11},{7,10},{8,5},{9,4},... | collective-permute-start | bytes 245768 | tf_op jit(solution)/shard_map/ppermute | solution.py:223
  11.2 4.7 %collective-permute-start.3 = (bf16[2,80,256]{2,1,0:T(8,128)(2,1)S(1)}, bf16[2,80,256]{2,1,0:T(8,128)(2,1)S(1)}, u32[]{:S(2)}, u32[]{:S(2)}) collective-permute-start(bf16[2,80,256]{2,1,0:T(8,128)(2,1)S(1)} %get-tuple-element.18), channel_id=1, source_target_pairs={{0,9},{1,8},{2,11},{3,10},{4,13},{5,12},{6,15},{7,14},{8,1},{9,0},... | collective-permute-start | bytes 245768 | tf_op jit(solution)/shard_map/ppermute | solution.py:223
  11.3 4.7 %collective-permute-start.4 = (bf16[2,80,256]{2,1,0:T(8,128)(2,1)S(1)}, bf16[2,80,256]{2,1,0:T(8,128)(2,1)S(1)}, u32[]{:S(2)}, u32[]{:S(2)}) collective-permute-start(bf16[2,80,256]{2,1,0:T(8,128)(2,1)S(1)} %get-tuple-element.17), channel_id=1, source_target_pairs={{0,5},{1,4},{2,7},{3,6},{4,1},{5,0},{6,3},{7,2},{8,13},{9,12},{10,... | collective-permute-start | bytes 245768 | tf_op jit(solution)/shard_map/ppermute | solution.py:223
  18.9 3.8 %collective-permute-start.5 = (f32[8,16,128]{2,1,0:T(8,128)S(1)}, f32[8,16,128]{2,1,0:T(8,128)S(1)}, u32[]{:S(2)}, u32[]{:S(2)}) collective-permute-start(f32[8,16,128]{2,1,0:T(8,128)S(1)} %get-tuple-element.13), channel_id=1, source_target_pairs={{0,3},{1,2},{2,1},{3,0},{4,7},{5,6},{6,5},{7,4},{8,11},{9,10},{10,... | collective-permute-start | bytes 196616 | tf_op jit(solution)/shard_map/ppermute | solution.py:223
  22.8 1.4 %collective-permute-start.6 = (f32[16]{0:T(128)S(1)}, f32[16]{0:T(128)S(1)}, u32[]{:S(2)}, u32[]{:S(2)}) collective-permute-start(f32[16]{0:T(128)S(1)} %get-tuple-element.15), channel_id=1, source_target_pairs={{0,1},{1,0},{2,3},{3,2},{4,5},{5,4},{6,7},{7,6},{8,9},{9,8},{10,11... | collective-permute-start | bytes 200 | tf_op jit(solution)/shard_map/ppermute | solution.py:223
  24.2 3.1 %collective-permute-start.7 = (f32[16]{0:T(128)S(1)}, f32[16]{0:T(128)S(1)}, u32[]{:S(2)}, u32[]{:S(2)}) collective-permute-start(f32[16]{0:T(128)S(1)} %max.9), channel_id=1, source_target_pairs={{0,5},{1,4},{2,7},{3,6},{4,1},{5,0},{6,3},{7,2},{8,13},{9,12},{10,... | collective-permute-start | bytes 200 | tf_op jit(solution)/shard_map/ppermute | solution.py:223
  27.3 3.3 %collective-permute-start.8 = (f32[16]{0:T(128)S(1)}, f32[16]{0:T(128)S(1)}, u32[]{:S(2)}, u32[]{:S(2)}) collective-permute-start(f32[16]{0:T(128)S(1)} %max.10), channel_id=1, source_target_pairs={{0,9},{1,8},{2,11},{3,10},{4,13},{5,12},{6,15},{7,14},{8,1},{9,0},... | collective-permute-start | bytes 200 | tf_op jit(solution)/shard_map/ppermute | solution.py:223

commit v4 on v3

--- a/solution.py
+++ b/solution.py
@@ -116,11 +116,10 @@
         mine, counts = [], []
         for m in range(2):
             of_node = (node == (2 * g + m).astype(F32)) & (honest == 1.0)
-            for a in (1.0, 0.0):
-                here = jnp.where(of_node & (arm == a), 1.0, 0.0)
-                mine.append(out * here)
-                counts.append(jnp.broadcast_to(here, (8, here.shape[1])))
-        return jnp.concatenate(mine + counts, axis=0)
+            arms = [jnp.where(of_node & (arm == a), 1.0, 0.0) for a in (1.0, 0.0)]
+            counts += [jnp.broadcast_to(here, (8, here.shape[1])) for here in arms]
+            mine += [out[w : w + 8] * here for w in range(0, weeks, 8) for here in arms]
+        return jnp.concatenate(counts + mine, axis=0)
 
     def step_rows(key, tile):
         steps = []
@@ -133,17 +132,15 @@
     def pair_gains(left, total):
         gains = []
         for m in range(2):
-            base, count = 2 * m * weeks, 4 * weeks + 16 * m
-            treated, control = left[base : base + weeks], left[base + weeks : base + 2 * weeks]
-            all_treated, all_control = total[base : base + weeks], total[base + weeks : base + 2 * weeks]
+            base, count = 32 + 2 * m * weeks, 16 * m
             lt, lc = left[count : count + 8], left[count + 8 : count + 16]
             rt, rc = total[count : count + 8] - lt, total[count + 8 : count + 16] - lc
             it, ic = 1.0 / (rt + 1.0), 1.0 / (rc + 1.0)
             at, ac = 1.0 / (lt + 1.0) + it, 1.0 / (lc + 1.0) + ic
             spread = None
-            for w in range(0, weeks, 8):
-                rng = slice(w, w + 8)
-                gap = (treated[rng] * at - all_treated[rng] * it) - (control[rng] * ac - all_control[rng] * ic)
+            for w in range(base, base + 2 * weeks, 16):
+                treated, control = slice(w, w + 8), slice(w + 8, w + 16)
+                gap = (left[treated] * at - total[treated] * it) - (left[control] * ac - total[control] * ic)
                 spread = gap * gap if spread is None else spread + gap * gap
             cl, cr = lt + lc, rt + rc
             balance = cl * cr / ((cl + cr + 1.0) * (cl + cr + 1.0))
@@ -151,11 +148,12 @@
         return gains
 
     def totals(mine):
-        return jnp.broadcast_to(jnp.sum(mine, axis=1, keepdims=True), (mine.shape[0], BINS))
-
-    def store(tile, rows, gain):
-        gain_ref[2 * tile, rows] = gain[:, : BINS // 2]
-        gain_ref[2 * tile + 1, rows] = gain[:, BINS // 2 :]
+        return jnp.broadcast_to(jnp.sum(mine, axis=1, keepdims=True), (mine.shape[0], BINS // 2))
+
+    def store(tile, nodes, left, total):
+        for h in range(2):
+            for m, gain in enumerate(pair_gains(left[:, h * BINS // 2 : (h + 1) * BINS // 2], total)):
+                gain_ref[2 * tile + h, nodes[m]] = gain
 
     strays = jnp.zeros((1, depth), F32)
     est = jnp.zeros((2 * NODES, weeks // 2), F32)
@@ -185,10 +183,9 @@
             est_units = est_units + hot
             mine = week_rows(jnp.int32(g), out, key)
             total = totals(mine)
-            for tile in range(per_owner):
-                left = dot(mine, step_rows(key, tile), NT)
-                for m, gain in enumerate(pair_gains(left, total)):
-                    store(tile, slice(2 * g + m, 2 * g + m + 1), gain)
+            lefts = [dot(mine, step_rows(key, tile), NT) for tile in range(per_owner)]
+            for tile, left in enumerate(lefts):
+                store(tile, [slice(2 * g + m, 2 * g + m + 1) for m in range(2)], left, total)
 
     units = jnp.sum(est_units, axis=1, keepdims=True)
     effect_ref[...] = est / (units + 1.0)
@@ -204,9 +201,8 @@
                     sums[...] += dot(mine, step_rows(keys[other], tile), NT)
                     return total + totals(mine)
 
-                total = lax.fori_loop(0, PAIRS, over_lanes, jnp.zeros(sums.shape, F32))
-                for m, gain in enumerate(pair_gains(sums[...], total)):
-                    store(tile, pl.ds(2 * g + m, 1), gain)
+                total = lax.fori_loop(0, PAIRS, over_lanes, jnp.zeros((sums.shape[0], BINS // 2), F32))
+                store(tile, [pl.ds(2 * g + m, 1) for m in range(2)], sums[...], total)
             return carry
 
         lax.fori_loop(0, PAIRS, over_pairs, 0)

time: 31.2 us -> 31 us (level)
  transfers between devices with their start and end apart: 9 -> 9, of which waited for: 7 -> 7; matrix products, arithmetic and copies ran while one was open for 4% -> 4% of each run, Pallas kernels for 4% -> 5%
where the time goes in v4:
time: 31 us; the launch traced here: 30.8 us
  starting transfers between devices  14.4 us (46%)
  waiting for transfers between devices  9.59 us (31%)
  Pallas kernels  4.21 us (14%)
  other arithmetic  1.27 us (4%)
  local copies, waits for them, and re-layouts  0.72 us (2%)
  between operations  0.69 us (2%)
    ppermute x9, starting transfers between devices, swap(): lax.ppermute(x, axis, [(i, i ^ bit) for i in range(lax.axis_size(axis))])  14.4 us
    ppermute x9, waiting for transfers between devices, swap(): lax.ppermute(x, axis, [(i, i ^ bit) for i in range(lax.axis_size(axis))])  9.59 us
    pallas_call x1, Pallas kernels, shards(): pl.pallas_call(functools.partial(gain_kernel, layout, per_owner, periods)...  2.67 us
    pallas_call x1, Pallas kernels, shards(): pl.pallas_call(functools.partial(place_kernel, owners), out_shape=(jax.Sh...  1.39 us
    dynamic_slice x1, local copies, waits for them, and re-layouts, shards(): lax.dynamic_slice_in_dim(gain[:per_owner], (lax.axis_index('period') >> 1...  0.69 us
  transfers between devices with their start and end apart: 9, of which 7 were waited for; matrix products, arithmetic and copies ran while one was open for 4% of the time, Pallas kernels for 5%

profile of v4, /device:TPU:0, one launch (start us, length us, event | category | flops | bytes accessed | tf_op | source)
XLA Modules:
  0.0 30.8 jit_solution(9218193769097236397)
XLA Ops:
  0.6 0.5 %collective-permute-start = (bf16[32,256]{1,0:T(8,128)(2,1)}, bf16[32,256]{1,0:T(8,128)(2,1)S(1)}, u32[]{:S(2)}, u32[]{:S(2)}) collective-permute-start(bf16[32,256]{1,0:T(8,128)(2,1)} %bitcast.14), channel_id=1, source_target_pairs={{0,1},{1,0},{2,3},{3,2},{4,5},{5,4},{6,7},{7,6},{8,9},{9,8},{10,11... | collective-permute-start | bytes 49160 | tf_op jit(solution)/shard_map/ppermute | solution.py:219
  1.1 1.4 %shard_map.85 = (bf16[256,256]{1,0:T(8,128)(2,1)S(1)}, f32[72,256]{1,0:T(8,128)S(1)}) custom-call(s32[64,256]{1,0:T(8,128)} %bitcast.13, s32[1,256]{1,0:T(1,128)} %bitcast.16, s32[1,256]{1,0:T(1,128)} %bitcast.17, s32[1,256]{1,0:T(1,128)} %bitcast.18, s32[16,32]{1,0:T(8,128)} %chosen_ref.1, bf16[32,256]{1,0:T(8,128)(2,1)} %bitcast.15), custom_call_target="tpu_custom_call" | custom-call | tf_op jit(solution)/shard_map/pallas_call | solution.py:226
  2.5 0.0 collective-permute-done.other_ref
  2.6 0.2 shard_map.86
  2.7 3.7 %collective-permute-start.1 = (bf16[104,256]{1,0:T(8,128)(2,1)S(1)}, bf16[104,256]{1,0:T(8,128)(2,1)S(1)}, u32[]{:S(2)}, u32[]{:S(2)}) collective-permute-start(bf16[104,256]{1,0:T(8,128)(2,1)S(1)} %get-tuple-element.12), channel_id=1, source_target_pairs={{0,17},{1,16},{2,19},{3,18},{4,21},{5,20},{6,23},{7,22},{8,25},{9,... | collective-permute-start | bytes 159752 | tf_op jit(solution)/shard_map/ppermute | solution.py:219
  6.5 2.2 %collective-permute-done.1 = bf16[104,256]{1,0:T(8,128)(2,1)S(1)} collective-permute-done((bf16[104,256]{1,0:T(8,128)(2,1)S(1)}, bf16[104,256]{1,0:T(8,128)(2,1)S(1)}, u32[]{:S(2)}, u32[]{:S(2)}) %collective-permute-start.1) | collective-permute-done | bytes 53280 | tf_op jit(solution)/shard_map/ppermute | solution.py:219
  8.7 2.6 %collective-permute-start.2 = (bf16[2,80,256]{2,1,0:T(8,128)(2,1)S(1)}, bf16[2,80,256]{2,1,0:T(8,128)(2,1)S(1)}, u32[]{:S(2)}, u32[]{:S(2)}) collective-permute-start(bf16[2,80,256]{2,1,0:T(8,128)(2,1)S(1)} %get-tuple-element.19), channel_id=1, source_target_pairs={{0,13},{1,12},{2,15},{3,14},{4,9},{5,8},{6,11},{7,10},{8,5},{9,4},... | collective-permute-start | bytes 245768 | tf_op jit(solution)/shard_map/ppermute | solution.py:219
  11.2 0.0 collective-permute-start.3
  11.3 1.5 %collective-permute-start.4 = (bf16[2,80,256]{2,1,0:T(8,128)(2,1)S(1)}, bf16[2,80,256]{2,1,0:T(8,128)(2,1)S(1)}, u32[]{:S(2)}, u32[]{:S(2)}) collective-permute-start(bf16[2,80,256]{2,1,0:T(8,128)(2,1)S(1)} %get-tuple-element.17), channel_id=1, source_target_pairs={{0,5},{1,4},{2,7},{3,6},{4,1},{5,0},{6,3},{7,2},{8,13},{9,12},{10,... | collective-permute-start | bytes 245768 | tf_op jit(solution)/shard_map/ppermute | solution.py:219
  12.7 1.4 %collective-permute-done.2.refs_2_ = bf16[2,80,256]{2,1,0:T(8,128)(2,1)S(1)} collective-permute-done((bf16[2,80,256]{2,1,0:T(8,128)(2,1)S(1)}, bf16[2,80,256]{2,1,0:T(8,128)(2,1)S(1)}, u32[]{:S(2)}, u32[]{:S(2)}) %collective-permute-start.2) | collective-permute-done | bytes 81952 | tf_op jit(solution)/shard_map/ppermute | solution.py:219
  14.1 1.9 %collective-permute-done.3.refs_3_ = bf16[2,80,256]{2,1,0:T(8,128)(2,1)S(1)} collective-permute-done((bf16[2,80,256]{2,1,0:T(8,128)(2,1)S(1)}, bf16[2,80,256]{2,1,0:T(8,128)(2,1)S(1)}, u32[]{:S(2)}, u32[]{:S(2)}) %collective-permute-start.3) | collective-permute-done | bytes 81952 | tf_op jit(solution)/shard_map/ppermute | solution.py:219
  16.0 0.0 collective-permute-done.4.refs_4_
  16.0 2.7 %shard_map.87 = (f32[8,16,128]{2,1,0:T(8,128)S(1)}, f32[32,32]{1,0:T(8,128)S(1)}) custom-call(bf16[1,104,256]{2,1,0:T(8,128)(2,1)S(1)} %bitcast.9, bf16[1,104,256]{2,1,0:T(8,128)(2,1)S(1)} %bitcast.12, bf16[2,80,256]{2,1,0:T(8,128)(2,1)S(1)} %collective-permute-done.2.refs_2_, bf16[2,80,256]{2,1,0:T(8,128)(2,1)S(1)} %collective-permute-done.3.refs_3_, ...), custom_call_target="tpu_custom_call" | custom-call | tf_op jit(solution)/shard_map/pallas_call | solution.py:270
  18.7 1.7 %collective-permute-start.5 = (f32[8,16,128]{2,1,0:T(8,128)S(1)}, f32[8,16,128]{2,1,0:T(8,128)S(1)}, u32[]{:S(2)}, u32[]{:S(2)}) collective-permute-start(f32[8,16,128]{2,1,0:T(8,128)S(1)} %get-tuple-element.13), channel_id=1, source_target_pairs={{0,3},{1,2},{2,1},{3,0},{4,7},{5,6},{6,5},{7,4},{8,11},{9,10},{10,... | collective-permute-start | bytes 196616 | tf_op jit(solution)/shard_map/ppermute | solution.py:219
  20.4 2.0 %collective-permute-done.5 = f32[8,16,128]{2,1,0:T(8,128)S(1)} collective-permute-done((f32[8,16,128]{2,1,0:T(8,128)S(1)}, f32[8,16,128]{2,1,0:T(8,128)S(1)}, u32[]{:S(2)}, u32[]{:S(2)}) %collective-permute-start.5) | collective-permute-done | bytes 65568 | tf_op jit(solution)/shard_map/ppermute | solution.py:219
  22.4 0.1 fusion.3
  22.6 0.6 %collective-permute-start.6 = (f32[16]{0:T(128)S(1)}, f32[16]{0:T(128)S(1)}, u32[]{:S(2)}, u32[]{:S(2)}) collective-permute-start(f32[16]{0:T(128)S(1)} %get-tuple-element.15), channel_id=1, source_target_pairs={{0,1},{1,0},{2,3},{3,2},{4,5},{5,4},{6,7},{7,6},{8,9},{9,8},{10,11... | collective-permute-start | bytes 200 | tf_op jit(solution)/shard_map/ppermute | solution.py:219
  23.1 0.6 %slice_subtract_fusion = f32[16,32]{1,0:T(8,128)} fusion(f32[32,32]{1,0:T(8,128)S(1)} %get-tuple-element.14), kind=kLoop, calls=%fused_computation.9 | loop fusion | flops 512 | bytes 6144 | tf_op jit(solution)/shard_map/sub | solution.py:298
  23.7 0.2 collective-permute-done.6
  24.0 1.8 %collective-permute-start.7 = (f32[16]{0:T(128)S(1)}, f32[16]{0:T(128)S(1)}, u32[]{:S(2)}, u32[]{:S(2)}) collective-permute-start(f32[16]{0:T(128)S(1)} %max.9), channel_id=1, source_target_pairs={{0,5},{1,4},{2,7},{3,6},{4,1},{5,0},{6,3},{7,2},{8,13},{9,12},{10,... | collective-permute-start | bytes 200 | tf_op jit(solution)/shard_map/ppermute | solution.py:219
  25.8 1.3 %collective-permute-done.7 = f32[16]{0:T(128)S(1)} collective-permute-done((f32[16]{0:T(128)S(1)}, f32[16]{0:T(128)S(1)}, u32[]{:S(2)}, u32[]{:S(2)}) %collective-permute-start.7) | collective-permute-done | bytes 96 | tf_op jit(solution)/shard_map/ppermute | solution.py:219
  27.1 1.9 %collective-permute-start.8 = (f32[16]{0:T(128)S(1)}, f32[16]{0:T(128)S(1)}, u32[]{:S(2)}, u32[]{:S(2)}) collective-permute-start(f32[16]{0:T(128)S(1)} %max.10), channel_id=1, source_target_pairs={{0,9},{1,8},{2,11},{3,10},{4,13},{5,12},{6,15},{7,14},{8,1},{9,0},... | collective-permute-start | bytes 200 | tf_op jit(solution)/shard_map/ppermute | solution.py:219
  29.0 0.7 %constant_dynamic-slice_fusion = f32[4,16,64]{2,1,0:T(8,128)} fusion(f32[4,16,128]{2,1,0:T(8,128)S(1)} %slice.56, s32[]{:T(128)S(6)} %select_n.3), kind=kLoop, calls=%fused_computation.10 | loop fusion | bytes 32772 | tf_op jit(solution)/shard_map/dynamic_slice | solution.py:291
  29.7 0.6 %collective-permute-done.8 = f32[16]{0:T(128)S(1)} collective-permute-done((f32[16]{0:T(128)S(1)}, f32[16]{0:T(128)S(1)}, u32[]{:S(2)}, u32[]{:S(2)}) %collective-permute-start.8) | collective-permute-done | bytes 96 | tf_op jit(solution)/shard_map/ppermute | solution.py:219
  30.3 0.5 %max.11 = f32[16]{0:T(128)} maximum(f32[16]{0:T(128)S(1)} %max.10, f32[16]{0:T(128)S(1)} %collective-permute-done.8) | non-fusion elementwise | flops 16 | bytes 192 | tf_op jit(solution)/shard_map/max | solution.py:296
  (8 shorter events, 0.1 us)
Async XLA Ops:
  0.6 1.9 %collective-permute-start = (bf16[32,256]{1,0:T(8,128)(2,1)}, bf16[32,256]{1,0:T(8,128)(2,1)S(1)}, u32[]{:S(2)}, u32[]{:S(2)}) collective-permute-start(bf16[32,256]{1,0:T(8,128)(2,1)} %bitcast.14), channel_id=1, source_target_pairs={{0,1},{1,0},{2,3},{3,2},{4,5},{5,4},{6,7},{7,6},{8,9},{9,8},{10,11... | collective-permute-start | bytes 49160 | tf_op jit(solution)/shard_map/ppermute | solution.py:219
  2.7 5.9 %collective-permute-start.1 = (bf16[104,256]{1,0:T(8,128)(2,1)S(1)}, bf16[104,256]{1,0:T(8,128)(2,1)S(1)}, u32[]{:S(2)}, u32[]{:S(2)}) collective-permute-start(bf16[104,256]{1,0:T(8,128)(2,1)S(1)} %get-tuple-element.12), channel_id=1, source_target_pairs={{0,17},{1,16},{2,19},{3,18},{4,21},{5,20},{6,23},{7,22},{8,25},{9,... | collective-permute-start | bytes 159752 | tf_op jit(solution)/shard_map/ppermute | solution.py:219
  8.7 5.4 %collective-permute-start.2 = (bf16[2,80,256]{2,1,0:T(8,128)(2,1)S(1)}, bf16[2,80,256]{2,1,0:T(8,128)(2,1)S(1)}, u32[]{:S(2)}, u32[]{:S(2)}) collective-permute-start(bf16[2,80,256]{2,1,0:T(8,128)(2,1)S(1)} %get-tuple-element.19), channel_id=1, source_target_pairs={{0,13},{1,12},{2,15},{3,14},{4,9},{5,8},{6,11},{7,10},{8,5},{9,4},... | collective-permute-start | bytes 245768 | tf_op jit(solution)/shard_map/ppermute | solution.py:219
  11.2 4.7 %collective-permute-start.3 = (bf16[2,80,256]{2,1,0:T(8,128)(2,1)S(1)}, bf16[2,80,256]{2,1,0:T(8,128)(2,1)S(1)}, u32[]{:S(2)}, u32[]{:S(2)}) collective-permute-start(bf16[2,80,256]{2,1,0:T(8,128)(2,1)S(1)} %get-tuple-element.18), channel_id=1, source_target_pairs={{0,9},{1,8},{2,11},{3,10},{4,13},{5,12},{6,15},{7,14},{8,1},{9,0},... | collective-permute-start | bytes 245768 | tf_op jit(solution)/shard_map/ppermute | solution.py:219
  11.3 4.7 %collective-permute-start.4 = (bf16[2,80,256]{2,1,0:T(8,128)(2,1)S(1)}, bf16[2,80,256]{2,1,0:T(8,128)(2,1)S(1)}, u32[]{:S(2)}, u32[]{:S(2)}) collective-permute-start(bf16[2,80,256]{2,1,0:T(8,128)(2,1)S(1)} %get-tuple-element.17), channel_id=1, source_target_pairs={{0,5},{1,4},{2,7},{3,6},{4,1},{5,0},{6,3},{7,2},{8,13},{9,12},{10,... | collective-permute-start | bytes 245768 | tf_op jit(solution)/shard_map/ppermute | solution.py:219
  18.7 3.8 %collective-permute-start.5 = (f32[8,16,128]{2,1,0:T(8,128)S(1)}, f32[8,16,128]{2,1,0:T(8,128)S(1)}, u32[]{:S(2)}, u32[]{:S(2)}) collective-permute-start(f32[8,16,128]{2,1,0:T(8,128)S(1)} %get-tuple-element.13), channel_id=1, source_target_pairs={{0,3},{1,2},{2,1},{3,0},{4,7},{5,6},{6,5},{7,4},{8,11},{9,10},{10,... | collective-permute-start | bytes 196616 | tf_op jit(solution)/shard_map/ppermute | solution.py:219
  22.6 1.4 %collective-permute-start.6 = (f32[16]{0:T(128)S(1)}, f32[16]{0:T(128)S(1)}, u32[]{:S(2)}, u32[]{:S(2)}) collective-permute-start(f32[16]{0:T(128)S(1)} %get-tuple-element.15), channel_id=1, source_target_pairs={{0,1},{1,0},{2,3},{3,2},{4,5},{5,4},{6,7},{7,6},{8,9},{9,8},{10,11... | collective-permute-start | bytes 200 | tf_op jit(solution)/shard_map/ppermute | solution.py:219
  24.0 3.1 %collective-permute-start.7 = (f32[16]{0:T(128)S(1)}, f32[16]{0:T(128)S(1)}, u32[]{:S(2)}, u32[]{:S(2)}) collective-permute-start(f32[16]{0:T(128)S(1)} %max.9), channel_id=1, source_target_pairs={{0,5},{1,4},{2,7},{3,6},{4,1},{5,0},{6,3},{7,2},{8,13},{9,12},{10,... | collective-permute-start | bytes 200 | tf_op jit(solution)/shard_map/ppermute | solution.py:219
  27.1 3.2 %collective-permute-start.8 = (f32[16]{0:T(128)S(1)}, f32[16]{0:T(128)S(1)}, u32[]{:S(2)}, u32[]{:S(2)}) collective-permute-start(f32[16]{0:T(128)S(1)} %max.10), channel_id=1, source_target_pairs={{0,9},{1,8},{2,11},{3,10},{4,13},{5,12},{6,15},{7,14},{8,1},{9,0},... | collective-permute-start | bytes 200 | tf_op jit(solution)/shard_map/ppermute | solution.py:219

commit v5 on v4

--- a/solution.py
+++ b/solution.py
@@ -258,13 +258,12 @@
         whole = jnp.concatenate([x for x, _ in held], axis=0)
         came = cross(part(whole, groups, 2 * groups, 4), groups)
         held = [(part(whole, 0, groups, 4), ids), (came, [k ^ groups for k in ids])]
-    ids = [k for _, some in held for k in some]
     layout = [some for _, some in held]
     blocks = [x for x, _ in held]
-    for k in (3, 2, 1):
-        send = jnp.concatenate([part(x, k, k + 1, key_rows - 4 - width) for x, _ in held], axis=0)
-        blocks.append(cross(send, k))
-        layout.append([i ^ k for i in ids])
+    for (x, some), order in zip(held, ((1, 3, 2), (1, 3, 2))):
+        for k in order:
+            blocks.append(cross(part(x, k, k + 1, key_rows - 4 - width), k))
+            layout.append([i ^ k for i in some])
 
     depth = owners * units // PAIRS
     gain, effect = pl.pallas_call(

time: 31 us -> 30.3 us (0.977)
  waiting for transfers between devices: 9.59 us -> 7.55 us
  starting transfers between devices: 14.4 us -> 15.7 us
    ppermute x9 -> x12, waiting for transfers between devices: 9.59 us -> 7.55 us  [swap(): lax.ppermute(x, axis, [(i, i ^ bit) for i in range(lax.axis_size(axis))])]
    ppermute x9 -> x12, starting transfers between devices: 14.4 us -> 15.7 us  [swap(): lax.ppermute(x, axis, [(i, i ^ bit) for i in range(lax.axis_size(axis))])]
  transfers between devices with their start and end apart: 9 -> 12, of which waited for: 7 -> 7; matrix products, arithmetic and copies ran while one was open for 4% -> 4% of each run, Pallas kernels for 5% -> 5%
where the time goes in v5:
time: 30.3 us; the launch traced here: 30.2 us
  starting transfers between devices  15.7 us (52%)
  waiting for transfers between devices  7.55 us (25%)
  Pallas kernels  4.21 us (14%)
  other arithmetic  1.27 us (4%)
  local copies, waits for them, and re-layouts  0.75 us (2%)
  between operations  0.7 us (2%)
    ppermute x12, starting transfers between devices, swap(): lax.ppermute(x, axis, [(i, i ^ bit) for i in range(lax.axis_size(axis))])  15.7 us
    ppermute x12, waiting for transfers between devices, swap(): lax.ppermute(x, axis, [(i, i ^ bit) for i in range(lax.axis_size(axis))])  7.55 us
    pallas_call x1, Pallas kernels, shards(): pl.pallas_call(functools.partial(gain_kernel, layout, per_owner, periods)...  2.67 us
    pallas_call x1, Pallas kernels, shards(): pl.pallas_call(functools.partial(place_kernel, owners), out_shape=(jax.Sh...  1.39 us
    dynamic_slice x1, local copies, waits for them, and re-layouts, shards(): lax.dynamic_slice_in_dim(gain[:per_owner], (lax.axis_index('period') >> 1...  0.69 us
  transfers between devices with their start and end apart: 12, of which 7 were waited for; matrix products, arithmetic and copies ran while one was open for 4% of the time, Pallas kernels for 5%

profile of v5, /device:TPU:0, one launch (start us, length us, event | category | flops | bytes accessed | tf_op | source)
XLA Modules:
  0.0 30.2 jit_solution(3311211825407843338)
XLA Ops:
  0.6 0.5 %collective-permute-start = (bf16[32,256]{1,0:T(8,128)(2,1)}, bf16[32,256]{1,0:T(8,128)(2,1)S(1)}, u32[]{:S(2)}, u32[]{:S(2)}) collective-permute-start(bf16[32,256]{1,0:T(8,128)(2,1)} %bitcast.14), channel_id=1, source_target_pairs={{0,1},{1,0},{2,3},{3,2},{4,5},{5,4},{6,7},{7,6},{8,9},{9,8},{10,11... | collective-permute-start | bytes 49160 | tf_op jit(solution)/shard_map/ppermute | solution.py:219
  1.1 1.4 %shard_map.85 = (bf16[256,256]{1,0:T(8,128)(2,1)S(1)}, f32[72,256]{1,0:T(8,128)S(1)}) custom-call(s32[64,256]{1,0:T(8,128)} %bitcast.13, s32[1,256]{1,0:T(1,128)} %bitcast.16, s32[1,256]{1,0:T(1,128)} %bitcast.17, s32[1,256]{1,0:T(1,128)} %bitcast.18, s32[16,32]{1,0:T(8,128)} %chosen_ref.1, bf16[32,256]{1,0:T(8,128)(2,1)} %bitcast.15), custom_call_target="tpu_custom_call" | custom-call | tf_op jit(solution)/shard_map/pallas_call | solution.py:226
  2.5 0.0 collective-permute-done.other_ref
  2.6 0.2 shard_map.86
  2.8 3.8 %collective-permute-start.1 = (bf16[104,256]{1,0:T(8,128)(2,1)S(1)}, bf16[104,256]{1,0:T(8,128)(2,1)S(1)}, u32[]{:S(2)}, u32[]{:S(2)}) collective-permute-start(bf16[104,256]{1,0:T(8,128)(2,1)S(1)} %get-tuple-element.12), channel_id=1, source_target_pairs={{0,17},{1,16},{2,19},{3,18},{4,21},{5,20},{6,23},{7,22},{8,25},{9,... | collective-permute-start | bytes 159752 | tf_op jit(solution)/shard_map/ppermute | solution.py:219
  6.5 1.2 %collective-permute-start.2 = (bf16[1,80,256]{2,1,0:T(8,128)(2,1)S(1)}, bf16[1,80,256]{2,1,0:T(8,128)(2,1)S(1)}, u32[]{:S(2)}, u32[]{:S(2)}) collective-permute-start(bf16[1,80,256]{2,1,0:T(8,128)(2,1)S(1)} %get-tuple-element.28), channel_id=1, source_target_pairs={{0,5},{1,4},{2,7},{3,6},{4,1},{5,0},{6,3},{7,2},{8,13},{9,12},{10,... | collective-permute-start | bytes 122888 | tf_op jit(solution)/shard_map/ppermute | solution.py:219
  7.7 1.6 %collective-permute-start.3 = (bf16[1,80,256]{2,1,0:T(8,128)(2,1)S(1)}, bf16[1,80,256]{2,1,0:T(8,128)(2,1)S(1)}, u32[]{:S(2)}, u32[]{:S(2)}) collective-permute-start(bf16[1,80,256]{2,1,0:T(8,128)(2,1)S(1)} %get-tuple-element.27), channel_id=1, source_target_pairs={{0,13},{1,12},{2,15},{3,14},{4,9},{5,8},{6,11},{7,10},{8,5},{9,4},... | collective-permute-start | bytes 122888 | tf_op jit(solution)/shard_map/ppermute | solution.py:219
  9.4 0.1 collective-permute-start.4
  9.4 0.0 collective-permute-done.1
  9.5 1.7 %collective-permute-start.5 = (bf16[1,80,256]{2,1,0:T(8,128)(2,1)S(1)}, bf16[1,80,256]{2,1,0:T(8,128)(2,1)S(1)}, u32[]{:S(2)}, u32[]{:S(2)}) collective-permute-start(bf16[1,80,256]{2,1,0:T(8,128)(2,1)S(1)} %get-tuple-element.25), channel_id=1, source_target_pairs={{0,5},{1,4},{2,7},{3,6},{4,1},{5,0},{6,3},{7,2},{8,13},{9,12},{10,... | collective-permute-start | bytes 122888 | tf_op jit(solution)/shard_map/ppermute | solution.py:219
  11.2 1.2 %collective-permute-start.6 = (bf16[1,80,256]{2,1,0:T(8,128)(2,1)S(1)}, bf16[1,80,256]{2,1,0:T(8,128)(2,1)S(1)}, u32[]{:S(2)}, u32[]{:S(2)}) collective-permute-start(bf16[1,80,256]{2,1,0:T(8,128)(2,1)S(1)} %get-tuple-element.24), channel_id=1, source_target_pairs={{0,13},{1,12},{2,15},{3,14},{4,9},{5,8},{6,11},{7,10},{8,5},{9,4},... | collective-permute-start | bytes 122888 | tf_op jit(solution)/shard_map/ppermute | solution.py:219
  12.3 0.0 collective-permute-done.2.refs_2_
  12.3 0.5 %collective-permute-start.7 = (bf16[1,80,256]{2,1,0:T(8,128)(2,1)S(1)}, bf16[1,80,256]{2,1,0:T(8,128)(2,1)S(1)}, u32[]{:S(2)}, u32[]{:S(2)}) collective-permute-start(bf16[1,80,256]{2,1,0:T(8,128)(2,1)S(1)} %get-tuple-element.23), channel_id=1, source_target_pairs={{0,9},{1,8},{2,11},{3,10},{4,13},{5,12},{6,15},{7,14},{8,1},{9,0},... | collective-permute-start | bytes 122888 | tf_op jit(solution)/shard_map/ppermute | solution.py:219
  12.9 0.0 collective-permute-done.3.refs_3_
  12.9 0.2 collective-permute-done.4.refs_4_
  13.0 0.1 collective-permute-done.5.refs_5_
  13.2 2.6 %collective-permute-done.6.refs_6_ = bf16[1,80,256]{2,1,0:T(8,128)(2,1)S(1)} collective-permute-done((bf16[1,80,256]{2,1,0:T(8,128)(2,1)S(1)}, bf16[1,80,256]{2,1,0:T(8,128)(2,1)S(1)}, u32[]{:S(2)}, u32[]{:S(2)}) %collective-permute-start.6) | collective-permute-done | bytes 40992 | tf_op jit(solution)/shard_map/ppermute | solution.py:219
  15.7 0.0 collective-permute-done.7.refs_7_
  15.8 2.7 %shard_map.87 = (f32[8,16,128]{2,1,0:T(8,128)S(1)}, f32[32,32]{1,0:T(8,128)S(1)}) custom-call(bf16[1,104,256]{2,1,0:T(8,128)(2,1)S(1)} %bitcast.9, bf16[1,104,256]{2,1,0:T(8,128)(2,1)S(1)} %bitcast.12, bf16[1,80,256]{2,1,0:T(8,128)(2,1)S(1)} %collective-permute-done.2.refs_2_, bf16[1,80,256]{2,1,0:T(8,128)(2,1)S(1)} %collective-permute-done.3.refs_3_, ...), custom_call_target="tpu_custom_call" | custom-call | tf_op jit(solution)/shard_map/pallas_call | solution.py:269
  18.4 1.7 %collective-permute-start.8 = (f32[8,16,128]{2,1,0:T(8,128)S(1)}, f32[8,16,128]{2,1,0:T(8,128)S(1)}, u32[]{:S(2)}, u32[]{:S(2)}) collective-permute-start(f32[8,16,128]{2,1,0:T(8,128)S(1)} %get-tuple-element.13), channel_id=1, source_target_pairs={{0,3},{1,2},{2,1},{3,0},{4,7},{5,6},{6,5},{7,4},{8,11},{9,10},{10,... | collective-permute-start | bytes 196616 | tf_op jit(solution)/shard_map/ppermute | solution.py:219
  20.1 2.2 %collective-permute-done.8 = f32[8,16,128]{2,1,0:T(8,128)S(1)} collective-permute-done((f32[8,16,128]{2,1,0:T(8,128)S(1)}, f32[8,16,128]{2,1,0:T(8,128)S(1)}, u32[]{:S(2)}, u32[]{:S(2)}) %collective-permute-start.8) | collective-permute-done | bytes 65568 | tf_op jit(solution)/shard_map/ppermute | solution.py:219
  22.3 0.1 fusion
  22.4 0.5 %collective-permute-start.9 = (f32[16]{0:T(128)S(1)}, f32[16]{0:T(128)S(1)}, u32[]{:S(2)}, u32[]{:S(2)}) collective-permute-start(f32[16]{0:T(128)S(1)} %get-tuple-element.15), channel_id=1, source_target_pairs={{0,1},{1,0},{2,3},{3,2},{4,5},{5,4},{6,7},{7,6},{8,9},{9,8},{10,11... | collective-permute-start | bytes 200 | tf_op jit(solution)/shard_map/ppermute | solution.py:219
  22.9 0.6 %slice_subtract_fusion = f32[16,32]{1,0:T(8,128)} fusion(f32[32,32]{1,0:T(8,128)S(1)} %get-tuple-element.14), kind=kLoop, calls=%fused_computation.6 | loop fusion | flops 512 | bytes 6144 | tf_op jit(solution)/shard_map/sub | solution.py:297
  23.5 0.2 collective-permute-done.9
  23.7 1.4 %collective-permute-start.10 = (f32[16]{0:T(128)S(1)}, f32[16]{0:T(128)S(1)}, u32[]{:S(2)}, u32[]{:S(2)}) collective-permute-start(f32[16]{0:T(128)S(1)} %max.9), channel_id=1, source_target_pairs={{0,5},{1,4},{2,7},{3,6},{4,1},{5,0},{6,3},{7,2},{8,13},{9,12},{10,... | collective-permute-start | bytes 200 | tf_op jit(solution)/shard_map/ppermute | solution.py:219
  25.1 1.6 %collective-permute-done.10 = f32[16]{0:T(128)S(1)} collective-permute-done((f32[16]{0:T(128)S(1)}, f32[16]{0:T(128)S(1)}, u32[]{:S(2)}, u32[]{:S(2)}) %collective-permute-start.10) | collective-permute-done | bytes 96 | tf_op jit(solution)/shard_map/ppermute | solution.py:219
  26.7 1.5 %collective-permute-start.11 = (f32[16]{0:T(128)S(1)}, f32[16]{0:T(128)S(1)}, u32[]{:S(2)}, u32[]{:S(2)}) collective-permute-start(f32[16]{0:T(128)S(1)} %max.10), channel_id=1, source_target_pairs={{0,9},{1,8},{2,11},{3,10},{4,13},{5,12},{6,15},{7,14},{8,1},{9,0},... | collective-permute-start | bytes 200 | tf_op jit(solution)/shard_map/ppermute | solution.py:219
  28.2 0.7 %constant_dynamic-slice_fusion = f32[4,16,64]{2,1,0:T(8,128)} fusion(f32[4,16,128]{2,1,0:T(8,128)S(1)} %slice.56, s32[]{:T(128)S(6)} %select_n.3), kind=kLoop, calls=%fused_computation.7 | loop fusion | bytes 32772 | tf_op jit(solution)/shard_map/dynamic_slice | solution.py:290
  28.9 0.7 %collective-permute-done.11 = f32[16]{0:T(128)S(1)} collective-permute-done((f32[16]{0:T(128)S(1)}, f32[16]{0:T(128)S(1)}, u32[]{:S(2)}, u32[]{:S(2)}) %collective-permute-start.11) | collective-permute-done | bytes 96 | tf_op jit(solution)/shard_map/ppermute | solution.py:219
  29.6 0.5 %max.11 = f32[16]{0:T(128)} maximum(f32[16]{0:T(128)S(1)} %max.10, f32[16]{0:T(128)S(1)} %collective-permute-done.11) | non-fusion elementwise | flops 16 | bytes 192 | tf_op jit(solution)/shard_map/max | solution.py:295
  (9 shorter events, 0.1 us)
Async XLA Ops:
  0.6 1.9 %collective-permute-start = (bf16[32,256]{1,0:T(8,128)(2,1)}, bf16[32,256]{1,0:T(8,128)(2,1)S(1)}, u32[]{:S(2)}, u32[]{:S(2)}) collective-permute-start(bf16[32,256]{1,0:T(8,128)(2,1)} %bitcast.14), channel_id=1, source_target_pairs={{0,1},{1,0},{2,3},{3,2},{4,5},{5,4},{6,7},{7,6},{8,9},{9,8},{10,11... | collective-permute-start | bytes 49160 | tf_op jit(solution)/shard_map/ppermute | solution.py:219
  2.8 6.7 %collective-permute-start.1 = (bf16[104,256]{1,0:T(8,128)(2,1)S(1)}, bf16[104,256]{1,0:T(8,128)(2,1)S(1)}, u32[]{:S(2)}, u32[]{:S(2)}) collective-permute-start(bf16[104,256]{1,0:T(8,128)(2,1)S(1)} %get-tuple-element.12), channel_id=1, source_target_pairs={{0,17},{1,16},{2,19},{3,18},{4,21},{5,20},{6,23},{7,22},{8,25},{9,... | collective-permute-start | bytes 159752 | tf_op jit(solution)/shard_map/ppermute | solution.py:219
  6.5 5.8 %collective-permute-start.2 = (bf16[1,80,256]{2,1,0:T(8,128)(2,1)S(1)}, bf16[1,80,256]{2,1,0:T(8,128)(2,1)S(1)}, u32[]{:S(2)}, u32[]{:S(2)}) collective-permute-start(bf16[1,80,256]{2,1,0:T(8,128)(2,1)S(1)} %get-tuple-element.28), channel_id=1, source_target_pairs={{0,5},{1,4},{2,7},{3,6},{4,1},{5,0},{6,3},{7,2},{8,13},{9,12},{10,... | collective-permute-start | bytes 122888 | tf_op jit(solution)/shard_map/ppermute | solution.py:219
  7.7 5.1 %collective-permute-start.3 = (bf16[1,80,256]{2,1,0:T(8,128)(2,1)S(1)}, bf16[1,80,256]{2,1,0:T(8,128)(2,1)S(1)}, u32[]{:S(2)}, u32[]{:S(2)}) collective-permute-start(bf16[1,80,256]{2,1,0:T(8,128)(2,1)S(1)} %get-tuple-element.27), channel_id=1, source_target_pairs={{0,13},{1,12},{2,15},{3,14},{4,9},{5,8},{6,11},{7,10},{8,5},{9,4},... | collective-permute-start | bytes 122888 | tf_op jit(solution)/shard_map/ppermute | solution.py:219
  9.4 3.7 %collective-permute-start.4 = (bf16[1,80,256]{2,1,0:T(8,128)(2,1)S(1)}, bf16[1,80,256]{2,1,0:T(8,128)(2,1)S(1)}, u32[]{:S(2)}, u32[]{:S(2)}) collective-permute-start(bf16[1,80,256]{2,1,0:T(8,128)(2,1)S(1)} %get-tuple-element.26), channel_id=1, source_target_pairs={{0,9},{1,8},{2,11},{3,10},{4,13},{5,12},{6,15},{7,14},{8,1},{9,0},... | collective-permute-start | bytes 122888 | tf_op jit(solution)/shard_map/ppermute | solution.py:219
  9.5 3.7 %collective-permute-start.5 = (bf16[1,80,256]{2,1,0:T(8,128)(2,1)S(1)}, bf16[1,80,256]{2,1,0:T(8,128)(2,1)S(1)}, u32[]{:S(2)}, u32[]{:S(2)}) collective-permute-start(bf16[1,80,256]{2,1,0:T(8,128)(2,1)S(1)} %get-tuple-element.25), channel_id=1, source_target_pairs={{0,5},{1,4},{2,7},{3,6},{4,1},{5,0},{6,3},{7,2},{8,13},{9,12},{10,... | collective-permute-start | bytes 122888 | tf_op jit(solution)/shard_map/ppermute | solution.py:219
  11.2 4.6 %collective-permute-start.6 = (bf16[1,80,256]{2,1,0:T(8,128)(2,1)S(1)}, bf16[1,80,256]{2,1,0:T(8,128)(2,1)S(1)}, u32[]{:S(2)}, u32[]{:S(2)}) collective-permute-start(bf16[1,80,256]{2,1,0:T(8,128)(2,1)S(1)} %get-tuple-element.24), channel_id=1, source_target_pairs={{0,13},{1,12},{2,15},{3,14},{4,9},{5,8},{6,11},{7,10},{8,5},{9,4},... | collective-permute-start | bytes 122888 | tf_op jit(solution)/shard_map/ppermute | solution.py:219
  12.3 3.4 %collective-permute-start.7 = (bf16[1,80,256]{2,1,0:T(8,128)(2,1)S(1)}, bf16[1,80,256]{2,1,0:T(8,128)(2,1)S(1)}, u32[]{:S(2)}, u32[]{:S(2)}) collective-permute-start(bf16[1,80,256]{2,1,0:T(8,128)(2,1)S(1)} %get-tuple-element.23), channel_id=1, source_target_pairs={{0,9},{1,8},{2,11},{3,10},{4,13},{5,12},{6,15},{7,14},{8,1},{9,0},... | collective-permute-start | bytes 122888 | tf_op jit(solution)/shard_map/ppermute | solution.py:219
  18.4 3.8 %collective-permute-start.8 = (f32[8,16,128]{2,1,0:T(8,128)S(1)}, f32[8,16,128]{2,1,0:T(8,128)S(1)}, u32[]{:S(2)}, u32[]{:S(2)}) collective-permute-start(f32[8,16,128]{2,1,0:T(8,128)S(1)} %get-tuple-element.13), channel_id=1, source_target_pairs={{0,3},{1,2},{2,1},{3,0},{4,7},{5,6},{6,5},{7,4},{8,11},{9,10},{10,... | collective-permute-start | bytes 196616 | tf_op jit(solution)/shard_map/ppermute | solution.py:219
  22.4 1.3 %collective-permute-start.9 = (f32[16]{0:T(128)S(1)}, f32[16]{0:T(128)S(1)}, u32[]{:S(2)}, u32[]{:S(2)}) collective-permute-start(f32[16]{0:T(128)S(1)} %get-tuple-element.15), channel_id=1, source_target_pairs={{0,1},{1,0},{2,3},{3,2},{4,5},{5,4},{6,7},{7,6},{8,9},{9,8},{10,11... | collective-permute-start | bytes 200 | tf_op jit(solution)/shard_map/ppermute | solution.py:219
  23.7 3.0 %collective-permute-start.10 = (f32[16]{0:T(128)S(1)}, f32[16]{0:T(128)S(1)}, u32[]{:S(2)}, u32[]{:S(2)}) collective-permute-start(f32[16]{0:T(128)S(1)} %max.9), channel_id=1, source_target_pairs={{0,5},{1,4},{2,7},{3,6},{4,1},{5,0},{6,3},{7,2},{8,13},{9,12},{10,... | collective-permute-start | bytes 200 | tf_op jit(solution)/shard_map/ppermute | solution.py:219
  26.7 3.0 %collective-permute-start.11 = (f32[16]{0:T(128)S(1)}, f32[16]{0:T(128)S(1)}, u32[]{:S(2)}, u32[]{:S(2)}) collective-permute-start(f32[16]{0:T(128)S(1)} %max.10), channel_id=1, source_target_pairs={{0,9},{1,8},{2,11},{3,10},{4,13},{5,12},{6,15},{7,14},{8,1},{9,0},... | collective-permute-start | bytes 200 | tf_op jit(solution)/shard_map/ppermute | solution.py:219

commit v6 on v4

--- a/solution.py
+++ b/solution.py
@@ -258,13 +258,22 @@
         whole = jnp.concatenate([x for x, _ in held], axis=0)
         came = cross(part(whole, groups, 2 * groups, 4), groups)
         held = [(part(whole, 0, groups, 4), ids), (came, [k ^ groups for k in ids])]
-    ids = [k for _, some in held for k in some]
     layout = [some for _, some in held]
     blocks = [x for x, _ in held]
+    def sent(x, k):
+        return part(x, k, k + 1, key_rows - 4 - width)
+
+    (kept, some), (came, others) = held
+    for k in (1, 2):
+        blocks.append(cross(sent(kept, k), k))
+        layout.append([i ^ k for i in some])
     for k in (3, 2, 1):
-        send = jnp.concatenate([part(x, k, k + 1, key_rows - 4 - width) for x, _ in held], axis=0)
-        blocks.append(cross(send, k))
-        layout.append([i ^ k for i in ids])
+        if k in (1, 2):
+            blocks.append(cross(sent(came, k), k))
+            layout.append([i ^ k for i in others])
+        else:
+            blocks.append(cross(jnp.concatenate([sent(kept, k), sent(came, k)], axis=0), k))
+            layout.append([i ^ k for i in some + others])
 
     depth = owners * units // PAIRS
     gain, effect = pl.pallas_call(
@@ -290,11 +299,11 @@
     share = BINS // periods
     gains = lax.dynamic_slice_in_dim(gain[:per_owner], (lax.axis_index("period") >> 1) * share, share, 2)
     best = jnp.max(gain, axis=(0, 2))
+    bit = half // 2
+    while bit:
+        best = jnp.maximum(best, cross(best, bit))
+        bit //= 2
     best = jnp.maximum(best, swap(best, "period", 1))
-    bit = 1
-    while bit < half:
-        best = jnp.maximum(best, cross(best, bit))
-        bit *= 2
     return gains, best, effect[:NODES] - effect[NODES:]
 
 

time: 31 us -> 30.1 us (0.971)
  waiting for transfers between devices: 9.59 us -> 6.92 us
  starting transfers between devices: 14.4 us -> 16 us
    ppermute x9 -> x11, waiting for transfers between devices: 9.59 us -> 6.92 us  [swap(): lax.ppermute(x, axis, [(i, i ^ bit) for i in range(lax.axis_size(axis))])]
    ppermute x9 -> x11, starting transfers between devices: 14.4 us -> 16 us  [swap(): lax.ppermute(x, axis, [(i, i ^ bit) for i in range(lax.axis_size(axis))])]
    max x2, other arithmetic: 0.52 us -> 0.01 us  [shards(): best = jnp.maximum(best, cross(best, bit))]
    max x1, other arithmetic: 0.01 us -> 0.51 us  [shards(): best = jnp.maximum(best, swap(best, 'period', 1))]
  transfers between devices with their start and end apart: 9 -> 11, of which waited for: 7 -> 6; matrix products, arithmetic and copies ran while one was open for 4% -> 4% of each run, Pallas kernels for 5% -> 5%
where the time goes in v6:
time: 30.1 us; the launch traced here: 29.9 us
  starting transfers between devices  16 us (53%)
  waiting for transfers between devices  6.92 us (23%)
  Pallas kernels  4.21 us (14%)
  other arithmetic  1.28 us (4%)
  local copies, waits for them, and re-layouts  0.75 us (2%)
  between operations  0.71 us (2%)
    ppermute x11, starting transfers between devices, swap(): lax.ppermute(x, axis, [(i, i ^ bit) for i in range(lax.axis_size(axis))])  16 us
    ppermute x11, waiting for transfers between devices, swap(): lax.ppermute(x, axis, [(i, i ^ bit) for i in range(lax.axis_size(axis))])  6.92 us
    pallas_call x1, Pallas kernels, shards(): pl.pallas_call(functools.partial(gain_kernel, layout, per_owner, periods)...  2.67 us
    pallas_call x1, Pallas kernels, shards(): pl.pallas_call(functools.partial(place_kernel, owners), out_shape=(jax.Sh...  1.39 us
    dynamic_slice x1, local copies, waits for them, and re-layouts, shards(): lax.dynamic_slice_in_dim(gain[:per_owner], (lax.axis_index('period') >> 1...  0.69 us
  transfers between devices with their start and end apart: 11, of which 6 were waited for; matrix products, arithmetic and copies ran while one was open for 4% of the time, Pallas kernels for 5%

profile of v6, /device:TPU:0, one launch (start us, length us, event | category | flops | bytes accessed | tf_op | source)
XLA Modules:
  0.0 29.9 jit_solution(11046602550739523273)
XLA Ops:
  0.6 0.5 %collective-permute-start = (bf16[32,256]{1,0:T(8,128)(2,1)}, bf16[32,256]{1,0:T(8,128)(2,1)S(1)}, u32[]{:S(2)}, u32[]{:S(2)}) collective-permute-start(bf16[32,256]{1,0:T(8,128)(2,1)} %bitcast.14), channel_id=1, source_target_pairs={{0,1},{1,0},{2,3},{3,2},{4,5},{5,4},{6,7},{7,6},{8,9},{9,8},{10,11... | collective-permute-start | bytes 49160 | tf_op jit(solution)/shard_map/ppermute | solution.py:219
  1.1 1.4 %shard_map.85 = (bf16[256,256]{1,0:T(8,128)(2,1)S(1)}, f32[72,256]{1,0:T(8,128)S(1)}) custom-call(s32[64,256]{1,0:T(8,128)} %bitcast.13, s32[1,256]{1,0:T(1,128)} %bitcast.16, s32[1,256]{1,0:T(1,128)} %bitcast.17, s32[1,256]{1,0:T(1,128)} %bitcast.18, s32[16,32]{1,0:T(8,128)} %chosen_ref.1, bf16[32,256]{1,0:T(8,128)(2,1)} %bitcast.15), custom_call_target="tpu_custom_call" | custom-call | tf_op jit(solution)/shard_map/pallas_call | solution.py:226
  2.5 0.0 collective-permute-done.other_ref
  2.6 0.2 shard_map.86
  2.8 3.8 %collective-permute-start.1 = (bf16[104,256]{1,0:T(8,128)(2,1)S(1)}, bf16[104,256]{1,0:T(8,128)(2,1)S(1)}, u32[]{:S(2)}, u32[]{:S(2)}) collective-permute-start(bf16[104,256]{1,0:T(8,128)(2,1)S(1)} %get-tuple-element.12), channel_id=1, source_target_pairs={{0,17},{1,16},{2,19},{3,18},{4,21},{5,20},{6,23},{7,22},{8,25},{9,... | collective-permute-start | bytes 159752 | tf_op jit(solution)/shard_map/ppermute | solution.py:219
  6.5 1.2 %collective-permute-start.2 = (bf16[1,80,256]{2,1,0:T(8,128)(2,1)S(1)}, bf16[1,80,256]{2,1,0:T(8,128)(2,1)S(1)}, u32[]{:S(2)}, u32[]{:S(2)}) collective-permute-start(bf16[1,80,256]{2,1,0:T(8,128)(2,1)S(1)} %get-tuple-element.26), channel_id=1, source_target_pairs={{0,5},{1,4},{2,7},{3,6},{4,1},{5,0},{6,3},{7,2},{8,13},{9,12},{10,... | collective-permute-start | bytes 122888 | tf_op jit(solution)/shard_map/ppermute | solution.py:219
  7.7 1.7 %collective-permute-start.3 = (bf16[1,80,256]{2,1,0:T(8,128)(2,1)S(1)}, bf16[1,80,256]{2,1,0:T(8,128)(2,1)S(1)}, u32[]{:S(2)}, u32[]{:S(2)}) collective-permute-start(bf16[1,80,256]{2,1,0:T(8,128)(2,1)S(1)} %get-tuple-element.25), channel_id=1, source_target_pairs={{0,9},{1,8},{2,11},{3,10},{4,13},{5,12},{6,15},{7,14},{8,1},{9,0},... | collective-permute-start | bytes 122888 | tf_op jit(solution)/shard_map/ppermute | solution.py:219
  9.4 0.0 collective-permute-done.1
  9.4 2.0 %collective-permute-start.4 = (bf16[2,80,256]{2,1,0:T(8,128)(2,1)S(1)}, bf16[2,80,256]{2,1,0:T(8,128)(2,1)S(1)}, u32[]{:S(2)}, u32[]{:S(2)}) collective-permute-start(bf16[2,80,256]{2,1,0:T(8,128)(2,1)S(1)} %maximum_maximum_fusion), channel_id=1, source_target_pairs={{0,13},{1,12},{2,15},{3,14},{4,9},{5,8},{6,11},{7,10},{8,5},{9,4},... | collective-permute-start | bytes 245768 | tf_op jit(solution)/shard_map/ppermute | solution.py:219
  11.4 0.1 collective-permute-start.5
  11.5 1.4 %collective-permute-start.6 = (bf16[1,80,256]{2,1,0:T(8,128)(2,1)S(1)}, bf16[1,80,256]{2,1,0:T(8,128)(2,1)S(1)}, u32[]{:S(2)}, u32[]{:S(2)}) collective-permute-start(bf16[1,80,256]{2,1,0:T(8,128)(2,1)S(1)} %get-tuple-element.23), channel_id=1, source_target_pairs={{0,5},{1,4},{2,7},{3,6},{4,1},{5,0},{6,3},{7,2},{8,13},{9,12},{10,... | collective-permute-start | bytes 122888 | tf_op jit(solution)/shard_map/ppermute | solution.py:219
  12.9 0.0 collective-permute-done.2.refs_2_
  12.9 0.0 collective-permute-done.3.refs_3_
  12.9 2.4 %collective-permute-done.5.refs_5_ = bf16[1,80,256]{2,1,0:T(8,128)(2,1)S(1)} collective-permute-done((bf16[1,80,256]{2,1,0:T(8,128)(2,1)S(1)}, bf16[1,80,256]{2,1,0:T(8,128)(2,1)S(1)}, u32[]{:S(2)}, u32[]{:S(2)}) %collective-permute-start.5) | collective-permute-done | bytes 40992 | tf_op jit(solution)/shard_map/ppermute | solution.py:219
  15.3 0.2 collective-permute-done.6.refs_6_
  15.4 0.0 collective-permute-done.4.refs_4_
  15.4 2.7 %shard_map.87 = (f32[8,16,128]{2,1,0:T(8,128)S(1)}, f32[32,32]{1,0:T(8,128)S(1)}) custom-call(bf16[1,104,256]{2,1,0:T(8,128)(2,1)S(1)} %bitcast.9, bf16[1,104,256]{2,1,0:T(8,128)(2,1)S(1)} %bitcast.12, bf16[1,80,256]{2,1,0:T(8,128)(2,1)S(1)} %collective-permute-done.2.refs_2_, bf16[1,80,256]{2,1,0:T(8,128)(2,1)S(1)} %collective-permute-done.3.refs_3_, ...), custom_call_target="tpu_custom_call" | custom-call | tf_op jit(solution)/shard_map/pallas_call | solution.py:279
  18.1 1.7 %collective-permute-start.7 = (f32[8,16,128]{2,1,0:T(8,128)S(1)}, f32[8,16,128]{2,1,0:T(8,128)S(1)}, u32[]{:S(2)}, u32[]{:S(2)}) collective-permute-start(f32[8,16,128]{2,1,0:T(8,128)S(1)} %get-tuple-element.13), channel_id=1, source_target_pairs={{0,3},{1,2},{2,1},{3,0},{4,7},{5,6},{6,5},{7,4},{8,11},{9,10},{10,... | collective-permute-start | bytes 196616 | tf_op jit(solution)/shard_map/ppermute | solution.py:219
  19.8 2.0 %collective-permute-done.7 = f32[8,16,128]{2,1,0:T(8,128)S(1)} collective-permute-done((f32[8,16,128]{2,1,0:T(8,128)S(1)}, f32[8,16,128]{2,1,0:T(8,128)S(1)}, u32[]{:S(2)}, u32[]{:S(2)}) %collective-permute-start.7) | collective-permute-done | bytes 65568 | tf_op jit(solution)/shard_map/ppermute | solution.py:219
  21.9 0.1 fusion
  22.0 2.0 %collective-permute-start.8 = (f32[16]{0:T(128)S(1)}, f32[16]{0:T(128)S(1)}, u32[]{:S(2)}, u32[]{:S(2)}) collective-permute-start(f32[16]{0:T(128)S(1)} %get-tuple-element.15), channel_id=1, source_target_pairs={{0,9},{1,8},{2,11},{3,10},{4,13},{5,12},{6,15},{7,14},{8,1},{9,0},... | collective-permute-start | bytes 200 | tf_op jit(solution)/shard_map/ppermute | solution.py:219
  24.0 0.6 %slice_subtract_fusion = f32[16,32]{1,0:T(8,128)} fusion(f32[32,32]{1,0:T(8,128)S(1)} %get-tuple-element.14), kind=kLoop, calls=%fused_computation.5 | loop fusion | flops 512 | bytes 6144 | tf_op jit(solution)/shard_map/sub | solution.py:307
  24.6 0.7 %collective-permute-done.8 = f32[16]{0:T(128)S(1)} collective-permute-done((f32[16]{0:T(128)S(1)}, f32[16]{0:T(128)S(1)}, u32[]{:S(2)}, u32[]{:S(2)}) %collective-permute-start.8) | collective-permute-done | bytes 96 | tf_op jit(solution)/shard_map/ppermute | solution.py:219
  25.3 1.5 %collective-permute-start.9 = (f32[16]{0:T(128)S(1)}, f32[16]{0:T(128)S(1)}, u32[]{:S(2)}, u32[]{:S(2)}) collective-permute-start(f32[16]{0:T(128)S(1)} %max.9), channel_id=1, source_target_pairs={{0,5},{1,4},{2,7},{3,6},{4,1},{5,0},{6,3},{7,2},{8,13},{9,12},{10,... | collective-permute-start | bytes 200 | tf_op jit(solution)/shard_map/ppermute | solution.py:219
  26.8 1.5 %collective-permute-done.9 = f32[16]{0:T(128)S(1)} collective-permute-done((f32[16]{0:T(128)S(1)}, f32[16]{0:T(128)S(1)}, u32[]{:S(2)}, u32[]{:S(2)}) %collective-permute-start.9) | collective-permute-done | bytes 96 | tf_op jit(solution)/shard_map/ppermute | solution.py:219
  28.3 0.3 %collective-permute-start.10 = (f32[16]{0:T(128)S(1)}, f32[16]{0:T(128)S(1)}, u32[]{:S(2)}, u32[]{:S(2)}) collective-permute-start(f32[16]{0:T(128)S(1)} %max.10), channel_id=1, source_target_pairs={{0,1},{1,0},{2,3},{3,2},{4,5},{5,4},{6,7},{7,6},{8,9},{9,8},{10,11... | collective-permute-start | bytes 200 | tf_op jit(solution)/shard_map/ppermute | solution.py:219
  28.6 0.7 %constant_dynamic-slice_fusion = f32[4,16,64]{2,1,0:T(8,128)} fusion(f32[4,16,128]{2,1,0:T(8,128)S(1)} %slice.56, s32[]{:T(128)S(6)} %select_n.3), kind=kLoop, calls=%fused_computation.6 | loop fusion | bytes 32772 | tf_op jit(solution)/shard_map/dynamic_slice | solution.py:300
  29.3 0.1 collective-permute-done.10
  29.4 0.5 %max.11 = f32[16]{0:T(128)} maximum(f32[16]{0:T(128)S(1)} %max.10, f32[16]{0:T(128)S(1)} %collective-permute-done.10) | non-fusion elementwise | flops 16 | bytes 192 | tf_op jit(solution)/shard_map/max | solution.py:306
  (10 shorter events, 0.1 us)
Async XLA Ops:
  0.6 1.9 %collective-permute-start = (bf16[32,256]{1,0:T(8,128)(2,1)}, bf16[32,256]{1,0:T(8,128)(2,1)S(1)}, u32[]{:S(2)}, u32[]{:S(2)}) collective-permute-start(bf16[32,256]{1,0:T(8,128)(2,1)} %bitcast.14), channel_id=1, source_target_pairs={{0,1},{1,0},{2,3},{3,2},{4,5},{5,4},{6,7},{7,6},{8,9},{9,8},{10,11... | collective-permute-start | bytes 49160 | tf_op jit(solution)/shard_map/ppermute | solution.py:219
  2.8 6.6 %collective-permute-start.1 = (bf16[104,256]{1,0:T(8,128)(2,1)S(1)}, bf16[104,256]{1,0:T(8,128)(2,1)S(1)}, u32[]{:S(2)}, u32[]{:S(2)}) collective-permute-start(bf16[104,256]{1,0:T(8,128)(2,1)S(1)} %get-tuple-element.12), channel_id=1, source_target_pairs={{0,17},{1,16},{2,19},{3,18},{4,21},{5,20},{6,23},{7,22},{8,25},{9,... | collective-permute-start | bytes 159752 | tf_op jit(solution)/shard_map/ppermute | solution.py:219
  6.5 6.3 %collective-permute-start.2 = (bf16[1,80,256]{2,1,0:T(8,128)(2,1)S(1)}, bf16[1,80,256]{2,1,0:T(8,128)(2,1)S(1)}, u32[]{:S(2)}, u32[]{:S(2)}) collective-permute-start(bf16[1,80,256]{2,1,0:T(8,128)(2,1)S(1)} %get-tuple-element.26), channel_id=1, source_target_pairs={{0,5},{1,4},{2,7},{3,6},{4,1},{5,0},{6,3},{7,2},{8,13},{9,12},{10,... | collective-permute-start | bytes 122888 | tf_op jit(solution)/shard_map/ppermute | solution.py:219
  7.7 5.2 %collective-permute-start.3 = (bf16[1,80,256]{2,1,0:T(8,128)(2,1)S(1)}, bf16[1,80,256]{2,1,0:T(8,128)(2,1)S(1)}, u32[]{:S(2)}, u32[]{:S(2)}) collective-permute-start(bf16[1,80,256]{2,1,0:T(8,128)(2,1)S(1)} %get-tuple-element.25), channel_id=1, source_target_pairs={{0,9},{1,8},{2,11},{3,10},{4,13},{5,12},{6,15},{7,14},{8,1},{9,0},... | collective-permute-start | bytes 122888 | tf_op jit(solution)/shard_map/ppermute | solution.py:219
  9.4 6.0 %collective-permute-start.4 = (bf16[2,80,256]{2,1,0:T(8,128)(2,1)S(1)}, bf16[2,80,256]{2,1,0:T(8,128)(2,1)S(1)}, u32[]{:S(2)}, u32[]{:S(2)}) collective-permute-start(bf16[2,80,256]{2,1,0:T(8,128)(2,1)S(1)} %maximum_maximum_fusion), channel_id=1, source_target_pairs={{0,13},{1,12},{2,15},{3,14},{4,9},{5,8},{6,11},{7,10},{8,5},{9,4},... | collective-permute-start | bytes 245768 | tf_op jit(solution)/shard_map/ppermute | solution.py:219
  11.4 3.9 %collective-permute-start.5 = (bf16[1,80,256]{2,1,0:T(8,128)(2,1)S(1)}, bf16[1,80,256]{2,1,0:T(8,128)(2,1)S(1)}, u32[]{:S(2)}, u32[]{:S(2)}) collective-permute-start(bf16[1,80,256]{2,1,0:T(8,128)(2,1)S(1)} %get-tuple-element.24), channel_id=1, source_target_pairs={{0,9},{1,8},{2,11},{3,10},{4,13},{5,12},{6,15},{7,14},{8,1},{9,0},... | collective-permute-start | bytes 122888 | tf_op jit(solution)/shard_map/ppermute | solution.py:219
  11.5 3.9 %collective-permute-start.6 = (bf16[1,80,256]{2,1,0:T(8,128)(2,1)S(1)}, bf16[1,80,256]{2,1,0:T(8,128)(2,1)S(1)}, u32[]{:S(2)}, u32[]{:S(2)}) collective-permute-start(bf16[1,80,256]{2,1,0:T(8,128)(2,1)S(1)} %get-tuple-element.23), channel_id=1, source_target_pairs={{0,5},{1,4},{2,7},{3,6},{4,1},{5,0},{6,3},{7,2},{8,13},{9,12},{10,... | collective-permute-start | bytes 122888 | tf_op jit(solution)/shard_map/ppermute | solution.py:219
  18.1 3.8 %collective-permute-start.7 = (f32[8,16,128]{2,1,0:T(8,128)S(1)}, f32[8,16,128]{2,1,0:T(8,128)S(1)}, u32[]{:S(2)}, u32[]{:S(2)}) collective-permute-start(f32[8,16,128]{2,1,0:T(8,128)S(1)} %get-tuple-element.13), channel_id=1, source_target_pairs={{0,3},{1,2},{2,1},{3,0},{4,7},{5,6},{6,5},{7,4},{8,11},{9,10},{10,... | collective-permute-start | bytes 196616 | tf_op jit(solution)/shard_map/ppermute | solution.py:219
  22.0 3.3 %collective-permute-start.8 = (f32[16]{0:T(128)S(1)}, f32[16]{0:T(128)S(1)}, u32[]{:S(2)}, u32[]{:S(2)}) collective-permute-start(f32[16]{0:T(128)S(1)} %get-tuple-element.15), channel_id=1, source_target_pairs={{0,9},{1,8},{2,11},{3,10},{4,13},{5,12},{6,15},{7,14},{8,1},{9,0},... | collective-permute-start | bytes 200 | tf_op jit(solution)/shard_map/ppermute | solution.py:219
  25.3 3.0 %collective-permute-start.9 = (f32[16]{0:T(128)S(1)}, f32[16]{0:T(128)S(1)}, u32[]{:S(2)}, u32[]{:S(2)}) collective-permute-start(f32[16]{0:T(128)S(1)} %max.9), channel_id=1, source_target_pairs={{0,5},{1,4},{2,7},{3,6},{4,1},{5,0},{6,3},{7,2},{8,13},{9,12},{10,... | collective-permute-start | bytes 200 | tf_op jit(solution)/shard_map/ppermute | solution.py:219
  28.3 1.1 %collective-permute-start.10 = (f32[16]{0:T(128)S(1)}, f32[16]{0:T(128)S(1)}, u32[]{:S(2)}, u32[]{:S(2)}) collective-permute-start(f32[16]{0:T(128)S(1)} %max.10), channel_id=1, source_target_pairs={{0,1},{1,0},{2,3},{3,2},{4,5},{5,4},{6,7},{7,6},{8,9},{9,8},{10,11... | collective-permute-start | bytes 200 | tf_op jit(solution)/shard_map/ppermute | solution.py:219
